TPU v7x, 512 devices: a whole 4x8x8 slice. The times are simulated.
512 devices in a mesh: wide: 64 (over z, y), lev: 8 (over x, core).
Axes of the slice: x: 4, y: 8, z: 8, core: 2. Of those that a mesh axis runs over, the one named last changes fastest.
Arguments:
- alpha: bfloat16 [64, 4, 64, 4096], P('wide', None, 'lev'), may hold values from -6 to 6
- ens: bfloat16 [64, 4, 64, 4096], P('wide', None, 'lev'), may hold values from -16 to 16
- htile: bfloat16 [8, 128, 128], replicated, may hold values from -0.1875 to 0.1875
- vloc: float32 [64, 9], replicated, may hold values from 0.1 to 0.55
- pattern: int32 [32, 8], replicated, may hold values from 0 to 31
- region_sizes: int32 [64], replicated, may hold values from 1 to 128, 4096 in all
- owner: int32 [64], replicated, may hold values from 0 to 63, each once
- cotangent: bfloat16 [4, 64, 8192], P(None, 'lev', 'wide'), may hold values from -6 to 6
Outputs:
- increment: bfloat16 [4, 64, 8192], P(None, 'lev', 'wide')
- gradient: bfloat16 [64, 4, 64, 4096], P('wide', None, 'lev')
Inputs may be any that keep to these rules, and one draw needn't show every extreme that they name: `region_sizes`: the entries sum to 4096; the largest equals 128. `owner`: each index of wide appears once. `pattern`: entries of a row may repeat.
All inputs are finite; a program needn't handle non-finite values.
Results may differ from a plain program's by a relative error of at most 0.008.
Values may be sent and summed in bfloat16 or wider, within the bound.
A program may use at most 128 MiB of HBM per device.

v0:
```python
import math

import jax
import jax.numpy as jnp
from jax import lax
from jax.sharding import PartitionSpec as P

VREACH = 4


def padded_2(block, sides, width):
    for axis, dim in sides:
        count = lax.axis_size(axis)
        forward = [(i, i + 1) for i in range(count - 1)]
        backward = [(target, source) for source, target in forward]
        low = lax.ppermute(
            lax.slice_in_dim(block, block.shape[dim] - width, None, axis=dim), axis, forward
        )
        high = lax.ppermute(lax.slice_in_dim(block, 0, width, axis=dim), axis, backward)
        block = jnp.concatenate([low, block, high], axis=dim)
    return block


def in_blocks(array, dim, peers):
    shape = array.shape
    blocks = array.reshape(*shape[:dim], peers, shape[dim] // peers, *shape[dim + 1 :])
    return jnp.moveaxis(blocks, dim, 0)


def sent_and_summed(array, axis, dim):
    peers = lax.axis_size(axis)
    blocks = lax.all_to_all(in_blocks(array, dim, peers), axis, 0, 0, tiled=True)
    return jnp.sum(blocks, axis=0)


def joined_along(blocks, dim):
    shape = list(blocks.shape[1:])
    shape[dim] *= blocks.shape[0]
    return jnp.moveaxis(blocks, 0, dim).reshape(shape)


def sent_to_all(array, axis):
    peers = lax.axis_size(axis)
    return lax.all_to_all(
        jnp.broadcast_to(array[None], (peers, *array.shape)), axis, 0, 0, tiled=True
    )


def collect(array, axis, dim):
    return joined_along(sent_to_all(array, axis), dim)


def slot_tables(region_sizes, owner, columns, region_max):
    region_ends = jnp.cumsum(region_sizes)
    region_starts = region_ends - region_sizes
    column_ids = jnp.arange(columns, dtype=jnp.int32)
    region_of = jnp.sum((region_ends[None, :] <= column_ids[:, None]).astype(jnp.int32), axis=1)
    slot_of = owner[region_of] * region_max + column_ids - region_starts[region_of]
    holder = jnp.argsort(owner)
    offsets = jnp.arange(region_max, dtype=jnp.int32)
    source = region_starts[holder][:, None] + offsets[None, :]
    valid_slot = offsets[None, :] < region_sizes[holder][:, None]
    source = jnp.where(valid_slot, source, 0).reshape(-1)
    return (slot_of, source, valid_slot.reshape(-1))


def spread_blocks(values, pattern, htile):
    slots = htile.shape[0]
    tile_width = htile.shape[1]
    blocks = values.shape[3] // tile_width
    flat_rows = values.reshape(-1, blocks, tile_width)
    block_ids = jnp.arange(blocks, dtype=jnp.int32)
    selected = []
    for k in range(slots):
        selector = (block_ids[:, None] == pattern[:, k][None, :]).astype(jnp.bfloat16)
        picked = jnp.einsum("rbi,bc->rci", flat_rows, selector, preferred_element_type=jnp.float32)
        selected.append(picked.astype(jnp.bfloat16))
    stacked = jnp.concatenate(selected, axis=2)
    stacked_tiles = htile.reshape(slots * tile_width, tile_width)
    summed = jnp.einsum("rck,kj->rcj", stacked, stacked_tiles, preferred_element_type=jnp.float32)
    return summed.reshape(values.shape).astype(jnp.bfloat16)


def gather_blocks(values, pattern, htile):
    slots = htile.shape[0]
    tile_width = htile.shape[1]
    blocks = values.shape[3] // tile_width
    flat_rows = values.reshape(-1, blocks, tile_width)
    block_ids = jnp.arange(blocks, dtype=jnp.int32)
    selected = []
    for k in range(slots):
        selector = (pattern[:, k][:, None] == block_ids[None, :]).astype(jnp.bfloat16)
        picked = jnp.einsum("rbi,bc->rci", flat_rows, selector, preferred_element_type=jnp.float32)
        selected.append(picked.astype(jnp.bfloat16))
    stacked = jnp.concatenate(selected, axis=2)
    stacked_tiles = jnp.transpose(htile, (0, 2, 1)).reshape(slots * tile_width, tile_width)
    summed = jnp.einsum("rck,kj->rcj", stacked, stacked_tiles, preferred_element_type=jnp.float32)
    return summed.reshape(values.shape).astype(jnp.bfloat16)


def level_window(vloc, levels_here, band_reach):
    first_level = lax.axis_index("lev") * levels_here
    padded = jnp.pad(vloc, ((band_reach, band_reach), (0, 0)))
    return lax.dynamic_slice_in_dim(padded, first_level, levels_here + 2 * band_reach, 0)


def mix_down(extended, window, band_reach, levels_here):
    shape_out = extended.shape[:2] + (levels_here,) + extended.shape[3:]
    summed = jnp.zeros(shape_out, jnp.float32)
    for offset in range(-band_reach, band_reach + 1):
        weight = window[band_reach : band_reach + levels_here, offset + band_reach]
        lower = band_reach + offset
        summed = summed + weight[None, None, :, None] * extended[
            :, :, lower : lower + levels_here
        ].astype(jnp.float32)
    return summed.astype(jnp.bfloat16)


def mix_up(extended, window, band_reach, levels_here):
    shape_out = extended.shape[:2] + (levels_here,) + extended.shape[3:]
    summed = jnp.zeros(shape_out, jnp.float32)
    for offset in range(-band_reach, band_reach + 1):
        lower = band_reach - offset
        weight = window[lower : lower + levels_here, offset + band_reach]
        summed = summed + weight[None, None, :, None] * extended[
            :, :, lower : lower + levels_here
        ].astype(jnp.float32)
    return summed.astype(jnp.bfloat16)


def body(alpha, ens, htile, vloc, pattern, region_sizes, owner, cotangent):
    band_reach = VREACH
    levels_here = alpha.shape[2]
    columns = alpha.shape[3]
    region_max = cotangent.shape[2]
    member_scale = 1.0 / math.sqrt(alpha.shape[0] * lax.axis_size("wide"))
    window = level_window(vloc, levels_here, band_reach)
    slot_of, source, valid_slot = slot_tables(region_sizes, owner, columns, region_max)
    spread_field = spread_blocks(alpha, pattern, htile)
    extended = padded_2(spread_field, (("lev", 2),), band_reach)
    localized = mix_down(extended, window, band_reach, levels_here)
    partial_value = jnp.sum(ens.astype(jnp.float32) * localized.astype(jnp.float32), axis=0)
    partial_slots = jnp.take(partial_value, source, axis=2) * valid_slot.astype(jnp.float32)
    region_total = sent_and_summed(partial_slots, "wide", 2)
    increment = (region_total * member_scale).astype(jnp.bfloat16)
    gathered = collect(cotangent, "wide", 2)
    cot_cols = jnp.take(gathered, slot_of, axis=2)
    scaled = (ens.astype(jnp.float32) * cot_cols.astype(jnp.float32)[None]).astype(jnp.bfloat16)
    extended_back = padded_2(scaled, (("lev", 2),), band_reach)
    adjoint_mix = mix_up(extended_back, window, band_reach, levels_here)
    gradient = gather_blocks(adjoint_mix, pattern, htile)
    return (increment, gradient)


def solution(mesh):
    placed = (
        P("wide", None, "lev", None),
        P("wide", None, "lev", None),
        P(),
        P(),
        P(),
        P(),
        P(),
        P(None, "lev", "wide"),
    )
    return jax.shard_map(
        body,
        mesh=mesh,
        in_specs=placed,
        out_specs=(P(None, "lev", "wide"), P("wide", None, "lev", None)),
        check_vma=False,
    )
```

profile of v0, /device:TPU:1, one launch (start us, length us, event | category | flops | bytes accessed | tf_op | source)
XLA Modules:
  0.0 299.9 jit_solution(14041289731024932369)
XLA Ops:
  0.6 1.0 copy.163
  1.6 1.0 slice_bitcast_fusion
  2.6 0.3 fusion.1
  2.9 0.3 fusion.3
  3.2 0.3 fusion.5
  3.5 0.3 fusion.7
  3.8 0.3 fusion.9
  4.1 0.3 fusion.11
  4.4 0.3 fusion.13
  4.7 0.3 fusion.15
  5.1 0.7 convolution_convert_fusion.9
  6.0 8.8 %collective-permute-start.1 = (bf16[1,4,4,4096]{3,2,1,0:T(4,128)(2,1)S(1)}, bf16[1,4,4,4096]{3,2,1,0:T(4,128)(2,1)S(1)}, u32[]{:S(2)}, u32[]{:S(2)}) collective-permute-start(bf16[1,4,4,4096]{3,2,1,0:T(4,128)(2,1)S(1)} %get-tuple-element.77), channel_id=1, source_target_pairs={{1,0},{2,1},{3,2},{4,3},{5,4},{6,5},{7,6},{9,8},{10,9},{11,10},{12... | collective-permute-start | bytes 393224 | tf_op jit(solution)/shard_map/ppermute | solution.py:19
  14.8 1.9 collective-permute-start
  16.7 0.9 broadcast_in_dim.33
  17.7 12.3 %all-to-all-start.1 = ((bf16[64,4,8,128]{3,2,1,0:T(8,128)(2,1)}), bf16[64,4,8,128]{3,2,1,0:T(8,128)(2,1)S(1)}, u32[]{:S(2)}, u32[]{:S(2)}) async-start(bf16[64,4,8,128]{3,2,1,0:T(8,128)(2,1)} %broadcast_in_dim.33), calls=%async_computation.1 | async-start | bytes 1048576 | tf_op jit(solution)/shard_map/all_to_all | solution.py:44
  30.4 2.0 sort.17
  32.4 0.8 gather_fusion
  33.2 0.8 gather_fusion.1
  34.2 0.7 fusion.102
  35.1 0.7 fusion.101
  35.8 0.7 fusion.100
  36.5 0.7 fusion.99
  37.2 0.7 fusion.98
  37.9 0.7 fusion.97
  38.6 0.7 fusion.96
  39.4 0.7 fusion.95
  40.2 4.5 %compare_select_fusion.5 = (s32[4096,1]{0,1:T(1,128)S(1)}, s32[4096,1]{0,1:T(1,128)S(1)}) fusion(s32[]{:T(128)} %bitcast.102, s32[]{:T(128)} %bitcast.103, s32[]{:T(128)} %bitcast.104, s32[]{:T(128)} %bitcast.105, s32[]{:T(128)} %bitcast.106, s32[]{:T(128)} %bitcast.108, s32[]{:T(128)} %bitcast.107, s32[4096,1]{0,1:T(1,128)S(1)} %bitcast.380), kind=kLoop, calls=%fused_computation.159 | loop fusion | flops 61440 | bytes 49180 | tf_op jit(solution)/shard_map/gather | solution.py:58
  44.7 2.9 compare_reduce_fusion.56
  47.6 4.4 %compare_select_fusion.6 = s32[4096,1]{0,1:T(1,128)S(1)} fusion(s32[4096,1]{0,1:T(1,128)S(1)} %get-tuple-element.73, s32[]{:T(128)} %bitcast.167, s32[]{:T(128)} %bitcast.168, s32[]{:T(128)} %bitcast.169, s32[]{:T(128)} %bitcast.170, s32[]{:T(128)} %bitcast.171, s32[]{:T(128)} %bitcast.173, s32[]{:T(128)} %bitcast.172), kind=kLoop, calls=%fused_computation.160 | loop fusion | flops 49152 | bytes 32796 | tf_op jit(solution)/shard_map/gather | solution.py:58
  52.0 71.3 %compare_and_fusion.1 = (pred[4096]{0:T(1024)(128)(4,1)S(1)}, s32[4096]{0:T(1024)S(1)}, s32[4096]{0:T(1024)S(1)}) fusion(pred[4096]{0:T(1024)(128)(4,1)S(1)} %get-tuple-element.68, pred[4096]{0:T(1024)(128)(4,1)S(1)} %get-tuple-element.67, pred[4096]{0:T(1024)(128)(4,1)S(1)} %get-tuple-element.66, pred[4096]{0:T(1024)(128)(4,1)S(1)} %get-tuple-element.65, ...), kind=kLoop, calls=%fused_computation.211 | loop fusion | flops 503808 | bytes 303560 | tf_op jit(solution)/shard_map/jit(_take)/and | solution.py:147
  124.1 0.9 fusion.32
  124.9 5.9 %copy.152 = f32[4,8,4096]{1,0,2:T(4,128)} copy(f32[4,8,4096]{2,1,0:T(8,128)S(1)} %fusion.32) | data formatting | bytes 1048576 | tf_op jit(solution)/shard_map/reduce_sum | solution.py:142
  130.8 63.1 %gather_fusion.2 = f32[8192,4,8]{2,1,0:T(4,128)} fusion(f32[4,8,4096]{1,0,2:T(4,128)} %copy.152, s32[8192]{0:T(1024)S(1)} %broadcast_clamp_fusion), kind=kCustom, calls=%fused_computation.2 | custom fusion | bytes 2129920 | tf_op jit(solution)/shard_map/jit(_take)/gather | solution.py:143
  193.9 12.1 %copy.153 = f32[4,8,64,128]{3,1,0,2:T(8,128)S(1)} copy(f32[4,8,64,128]{1,0,3,2:T(4,128)} %bitcast.368) | data formatting | bytes 2097152 | tf_op jit(solution)/shard_map/jit(_take)/gather | solution.py:143
  206.1 8.1 %copy.160 = bf16[4,8,64,128]{1,0,3,2:T(4,128)(2,1)} copy(bf16[4,8,64,128]{3,1,0,2:T(8,128)(2,1)S(1)} %bitcast.370) | data formatting | bytes 1048576 | tf_op jit(solution)/shard_map/reshape | solution.py:39
  214.2 31.8 %gather_fusion.3 = bf16[4096,4,8]{2,1,0:T(4,128)(2,1)} fusion(bf16[4,8,8192]{1,0,2:T(4,128)(2,1)} %bitcast.369, s32[4096]{0:T(1024)S(1)} %broadcast_clamp_fusion.1), kind=kCustom, calls=%fused_computation.3 | custom fusion | bytes 540672 | tf_op jit(solution)/shard_map/jit(_take)/gather | solution.py:147
  246.0 5.4 %copy.157 = bf16[4096,4,8]{0,2,1:T(8,128)(2,1)S(1)} copy(bf16[4096,4,8]{2,1,0:T(4,128)(2,1)} %gather_fusion.3) | data formatting | bytes 524288 | tf_op jit(solution)/shard_map/jit(_take)/gather | solution.py:147
  251.6 2.7 collective-permute-start.3
  254.3 1.9 collective-permute-start.2
  256.2 1.2 multiply_bitcast_fusion
  257.4 12.5 %all-to-all-start = ((f32[64,4,8,128]{3,2,1,0:T(8,128)}), f32[64,4,8,128]{3,2,1,0:T(8,128)S(1)}, u32[]{:S(2)}, u32[]{:S(2)}) async-start(f32[64,4,8,128]{3,2,1,0:T(8,128)} %multiply_bitcast_fusion), calls=%async_computation | async-start | bytes 2097152 | tf_op jit(solution)/shard_map/all_to_all | solution.py:32
  269.9 1.0 fusion.43
  271.4 0.2 fusion.21
  271.7 0.2 fusion.23
  272.9 0.7 convolution_convert_fusion
  273.6 0.8 convert_element_type.309
  274.4 24.8 %all-to-all-done = f32[64,4,8,128]{3,2,1,0:T(8,128)S(1)} async-done(((f32[64,4,8,128]{3,2,1,0:T(8,128)}), f32[64,4,8,128]{3,2,1,0:T(8,128)S(1)}, u32[]{:S(2)}, u32[]{:S(2)}) %all-to-all-start) | async-done | bytes 1048608 | tf_op jit(solution)/shard_map/all_to_all | solution.py:32
  299.3 0.6 multiply_convert_fusion
  (49 shorter events, 3.4 us)
Async XLA Ops:
  2.6 2.4 copy-start.3
  4.7 12.0 %copy-start.5 = (bf16[4,8,128]{2,1,0:T(8,128)(2,1)S(1)}, bf16[4,8,128]{2,1,0:T(8,128)(2,1)}, u32[]{:S(2)}) copy-start(bf16[4,8,128]{2,1,0:T(8,128)(2,1)} %param.15) | copy-start | bytes 24580
  5.8 24.3 %copy-start = (s32[64]{0:T(128)S(1)}, s32[64]{0:T(128)}, u32[]{:S(2)}) copy-start(s32[64]{0:T(128)} %param.13) | copy-start | bytes 772
  5.8 24.6 %copy-start.1 = (s32[64]{0:T(128)S(1)}, s32[64]{0:T(128)}, u32[]{:S(2)}) copy-start(s32[64]{0:T(128)} %param.14) | copy-start | bytes 772
  6.0 117.9 %collective-permute-start.1 = (bf16[1,4,4,4096]{3,2,1,0:T(4,128)(2,1)S(1)}, bf16[1,4,4,4096]{3,2,1,0:T(4,128)(2,1)S(1)}, u32[]{:S(2)}, u32[]{:S(2)}) collective-permute-start(bf16[1,4,4,4096]{3,2,1,0:T(4,128)(2,1)S(1)} %get-tuple-element.77), channel_id=1, source_target_pairs={{1,0},{2,1},{3,2},{4,3},{5,4},{6,5},{7,6},{9,8},{10,9},{11,10},{12... | collective-permute-start | bytes 393224 | tf_op jit(solution)/shard_map/ppermute | solution.py:19
  14.8 109.2 %collective-permute-start = (bf16[1,4,4,4096]{3,2,1,0:T(4,128)(2,1)S(1)}, bf16[1,4,4,4096]{3,2,1,0:T(4,128)(2,1)S(1)}, u32[]{:S(2)}, u32[]{:S(2)}) collective-permute-start(bf16[1,4,4,4096]{3,2,1,0:T(4,128)(2,1)S(1)} %get-tuple-element.76), channel_id=1, source_target_pairs={{0,1},{1,2},{2,3},{3,4},{4,5},{5,6},{6,7},{8,9},{9,10},{10,11},{11... | collective-permute-start | bytes 393224 | tf_op jit(solution)/shard_map/ppermute | solution.py:16
  17.7 105.7 %copy-start.4 = (f32[64,9]{0,1:T(8,128)S(1)}, f32[64,9]{0,1:T(8,128)}, u32[]{:S(2)}) copy-start(f32[64,9]{0,1:T(8,128)} %param.11) | copy-start | bytes 6916
  17.7 188.4 %all-to-all-start.1 = ((bf16[64,4,8,128]{3,2,1,0:T(8,128)(2,1)}), bf16[64,4,8,128]{3,2,1,0:T(8,128)(2,1)S(1)}, u32[]{:S(2)}, u32[]{:S(2)}) async-start(bf16[64,4,8,128]{3,2,1,0:T(8,128)(2,1)} %broadcast_in_dim.33), calls=%async_computation.1 | async-start | bytes 1048576 | tf_op jit(solution)/shard_map/all_to_all | solution.py:44
  30.0 94.0 %copy-start.2 = (bf16[1,4,8,4096]{3,2,1,0:T(8,128)(2,1)S(1)}, bf16[1,4,8,4096]{3,2,1,0:T(8,128)(2,1)}, u32[]{:S(2)}) copy-start(bf16[1,4,8,4096]{3,2,1,0:T(8,128)(2,1)} %param.9) | copy-start | bytes 786436
  251.6 18.3 %collective-permute-start.3 = (bf16[1,4,4,4096]{3,2,1,0:T(4,128)(2,1)S(1)}, bf16[1,4,4,4096]{3,2,1,0:T(4,128)(2,1)S(1)}, u32[]{:S(2)}, u32[]{:S(2)}) collective-permute-start(bf16[1,4,4,4096]{3,2,1,0:T(4,128)(2,1)S(1)} %get-tuple-element.75), channel_id=1, source_target_pairs={{0,1},{1,2},{2,3},{3,4},{4,5},{5,6},{6,7},{8,9},{9,10},{10,11},{11... | collective-permute-start | bytes 393224 | tf_op jit(solution)/shard_map/ppermute | solution.py:16
  254.3 15.6 %collective-permute-start.2 = (bf16[1,4,4,4096]{3,2,1,0:T(4,128)(2,1)S(1)}, bf16[1,4,4,4096]{3,2,1,0:T(4,128)(2,1)S(1)}, u32[]{:S(2)}, u32[]{:S(2)}) collective-permute-start(bf16[1,4,4,4096]{3,2,1,0:T(4,128)(2,1)S(1)} %get-tuple-element.74), channel_id=1, source_target_pairs={{1,0},{2,1},{3,2},{4,3},{5,4},{6,5},{7,6},{9,8},{10,9},{11,10},{12... | collective-permute-start | bytes 393224 | tf_op jit(solution)/shard_map/ppermute | solution.py:19
  257.4 41.8 %all-to-all-start = ((f32[64,4,8,128]{3,2,1,0:T(8,128)}), f32[64,4,8,128]{3,2,1,0:T(8,128)S(1)}, u32[]{:S(2)}, u32[]{:S(2)}) async-start(f32[64,4,8,128]{3,2,1,0:T(8,128)} %multiply_bitcast_fusion), calls=%async_computation | async-start | bytes 2097152 | tf_op jit(solution)/shard_map/all_to_all | solution.py:32
where the time goes:
time: 302 us; the launch traced here: 300 us
  local copies, waits for them, and re-layouts  138 us (46%)
  other arithmetic  89.8 us (30%)
  starting transfers between devices  40.1 us (13%)
  waiting for transfers between devices  24.8 us (8%)
  matrix products  5.61 us (2%)
    gather x2, local copies, waits for them, and re-layouts, body(): jnp.take(partial_value, source, axis=2) * valid_slot.astype(jnp.float32)  75.2 us
    and x1, other arithmetic, body(): cot_cols = jnp.take(gathered, slot_of, axis=2)  71.3 us
    gather x2, local copies, waits for them, and re-layouts, body(): cot_cols = jnp.take(gathered, slot_of, axis=2)  37.2 us
    all_to_all x1, waiting for transfers between devices, sent_and_summed(): lax.all_to_all(in_blocks(array, dim, peers), axis, 0, 0, tiled=True)  24.8 us
    all_to_all x1, starting transfers between devices, sent_and_summed(): lax.all_to_all(in_blocks(array, dim, peers), axis, 0, 0, tiled=True)  12.5 us
    all_to_all x1, starting transfers between devices, sent_to_all(): lax.all_to_all(jnp.broadcast_to(array[None], (peers, *array.shape)), axis...  12.3 us
    ppermute x2, starting transfers between devices, padded_2(): lax.ppermute(lax.slice_in_dim(block, 0, width, axis=dim), axis, backward)  10.7 us
    reshape x1, local copies, waits for them, and re-layouts, joined_along(): return jnp.moveaxis(blocks, 0, dim).reshape(shape)  8.12 us
  transfers between devices with their start and end apart: 6, of which 1 were waited for; matrix products, arithmetic and copies ran while one was open for 61% of the time, Pallas kernels for 0%

commit v1 on v0

v1 whole, which is shorter than its diff:
```python
import functools
import math

import jax
import jax.numpy as jnp
from jax import lax
from jax.experimental import pallas as pl
from jax.experimental.pallas import tpu as pltpu
from jax.sharding import PartitionSpec as P

REACH = 4
MESH = pl.DeviceIdType.MESH
F32 = jnp.float32
BF16 = jnp.bfloat16
I32 = jnp.int32
VMEM_LIMIT = 60 * 1024 * 1024


def iota(shape, dim):
    return lax.broadcasted_iota(I32, shape, dim)


def halves_of(fields):
    first = iota(fields[0].shape, 0) < 4
    low, high = [], []
    for a, b in (fields[0:2], fields[2:4]):
        low.append(jnp.where(first, a, pltpu.roll(b, 4, 0)))
        high.append(jnp.where(first, pltpu.roll(a, 4, 0), b))
    return jnp.concatenate(low + high, axis=0)


def fields_of(rows):
    fields = []
    for pair in range(2):
        low = rows[8 * pair : 8 * pair + 8]
        high = rows[16 + 8 * pair : 24 + 8 * pair]
        first = iota(low.shape, 0) < 4
        fields.append(jnp.where(first, low, pltpu.roll(high, 4, 0)))
        fields.append(jnp.where(first, pltpu.roll(low, 4, 0), high))
    return fields


def kernel(
    side, n_lev, blocks, slots, members, width,
    alpha_h, ens_h, htile_h, vloc_h, pattern_h, sizes_h, owner_h, cot_h,
    inc_h, grad_h,
    alpha_v, ens_v, tile_v, vloc_v, pat_v, size_v, own_v, cot_v, tab_v, tab_s,
    a3, x, tiles_nt, band_v, ens_f, e1, e2, p3, h0, h1, r0, r1, q0, q1, q0f, q1f, t0, t1,
    g0, g1, snap, mixed, run, grad_v, inc_v,
    local_sem, out_sem, ag1_s, ag1_r, ag2_s, ag2_r, rs1_s, rs1_r, rs2_s, rs2_r, up_s, up_r, dn_s, dn_r,
    bup_s, bup_r, bdn_s, bdn_r,
):
    n_wide = side * side
    w_me, l_me = lax.axis_index("wide"), lax.axis_index("lev")
    z_me, y_me = w_me // side, w_me % side
    upper, lower = lax.rem(l_me + 1, n_lev), lax.rem(l_me + n_lev - 1, n_lev)
    steps = range(1, side)

    def along_y(d):
        return lax.rem(y_me + d, side)

    def along_z(d):
        return lax.rem(z_me + d, side)

    def at_y(y):
        return (z_me * side + y, l_me)

    def at_z(z):
        return (z * side + y_me, l_me)

    def remote(src, dst, s, r, device):
        return pltpu.make_async_remote_copy(
            src_ref=src, dst_ref=dst, send_sem=s, recv_sem=r, device_id=device, device_id_type=MESH
        )

    with jax.named_scope("load_and_greet"):
        loads = [
            pltpu.make_async_copy(src, dst, local_sem.at[i])
            for i, (src, dst) in enumerate(
                (
                    (sizes_h, size_v), (owner_h, own_v), (pattern_h, pat_v), (cot_h, cot_v),
                    (alpha_h, alpha_v), (htile_h, tile_v), (vloc_h, vloc_v), (ens_h, ens_v),
                )
            )
        ]
        for load in loads:
            load.start()
        barrier = pltpu.get_barrier_semaphore()
        friends = [at_y(along_y(d)) for d in steps] + [at_z(along_z(d)) for d in steps]
        friends += [(w_me, upper), (w_me, lower)]
        for friend in friends:
            pl.semaphore_signal(barrier, inc=1, device_id=friend, device_id_type=MESH)

    with jax.named_scope("tables"):
        for load in loads[:4]:
            load.wait()
        square = (n_wide, n_wide)
        rows, cols = iota(square, 0), iota(square, 1)
        size_b = jnp.broadcast_to(size_v[...], square)
        own_b = jnp.broadcast_to(own_v[...], square)
        start_c = jnp.sum(jnp.where(cols < rows, size_b, 0), axis=1, keepdims=True)
        size_c = jnp.sum(jnp.where(cols == rows, size_b, 0), axis=1, keepdims=True)
        own_c = jnp.sum(jnp.where(cols == rows, own_b, 0), axis=1, keepdims=True)
        held = own_c == cols
        base = 3 * slots
        tab_v[base : base + 1, 0:n_wide] = jnp.sum(jnp.where(held, start_c, 0), axis=0, keepdims=True)
        tab_v[base + 1 : base + 2, 0:n_wide] = jnp.sum(jnp.where(held, size_c, 0), axis=0, keepdims=True)
        tab_v[base + 2 : base + 3, 0:n_wide] = jnp.sum(jnp.where(cols == rows, start_c, 0), axis=0, keepdims=True)
        tab_v[base + 3 : base + 4, 0:n_wide] = size_v[...]
        tab_v[base + 4 : base + 5, 0:n_wide] = own_v[...]
        ends = iota((n_wide, blocks), 1) * 128 + 127
        covered = jnp.sum(jnp.where(start_c + size_c <= ends, 1, 0), axis=0, keepdims=True)
        tab_v[base + 5 : base + 6, 0:blocks] = jnp.minimum(covered, n_wide - 1)
        here, there = iota((blocks, blocks), 0), iota((blocks, blocks), 1)
        for k in range(slots):
            row = pat_v[k : k + 1, :]
            col = jnp.sum(jnp.where(here == there, row, 0), axis=1, keepdims=True)
            tab_v[k : k + 1, 0:blocks] = row
            before = jnp.max(jnp.where((col == row) & (here < there), here, -1), axis=0, keepdims=True)
            tab_v[slots + k : slots + k + 1, 0:blocks] = jnp.where(before < 0, blocks, before)
            last = jnp.max(jnp.where(col == there, here, -1), axis=0, keepdims=True)
            tab_v[2 * slots + k : 2 * slots + k + 1, 0:blocks] = jnp.where(last < 0, blocks, last)
        to_s = pltpu.make_async_copy(tab_v, tab_s, local_sem.at[8])
        to_s.start()
        to_s.wait()
        my_start = tab_s[base, w_me]
        my_size = tab_s[base + 1, w_me]
        my_off = my_start & 127

    lane16 = iota((16, 128), 1)
    lane32 = iota((32, 128), 1)

    with jax.named_scope("cotangent_stage_1"):
        cot = cot_v[...].astype(F32)
        tile = pltpu.roll(halves_of([cot[f] for f in range(4)]), my_off, 1)
        g0[w_me] = tile[:16].astype(BF16)
        g1[y_me * side + z_me] = tile[16:].astype(BF16)
        pl.semaphore_wait(barrier, len(friends))
        i0, i1 = w_me, y_me * side + z_me
        ag1 = []
        for d in steps:
            ag1.append(remote(g0.at[i0], g0.at[i0], ag1_s.at[0, d - 1], ag1_r.at[0, d - 1], at_y(along_y(d))))
            ag1.append(remote(g1.at[i1], g1.at[i1], ag1_s.at[1, d - 1], ag1_r.at[1, d - 1], at_z(along_z(d))))
        for copy in ag1:
            copy.start()

    def block_lanes(b):
        return pl.ds(pl.multiple_of(b * 128, 128), 128)

    with jax.named_scope("spread"):
        loads[4].wait()

        def split_alpha(b, _):
            a = alpha_v[0, :, :, block_lanes(b)].astype(F32)
            a3[b] = halves_of([a[f] for f in range(4)]).astype(BF16)
            return 0

        lax.fori_loop(0, blocks, split_alpha, 0, unroll=4)
        loads[5].wait()
        stacked = tile_v[...].reshape(slots * 128, 128)
        group = min(8, blocks)
        n_groups = blocks // group
        halo1 = []
        ag2 = []
        for c in range(n_groups):

            def pick(i, _, c=c):
                b = c * group + i
                at = pl.ds(pl.multiple_of(b * 32, 32), 32)
                for k in range(slots):
                    x[at, k * 128 : (k + 1) * 128] = a3[tab_s[k, b]]
                return 0

            lax.fori_loop(0, group, pick, 0, unroll=2)
            part = jnp.dot(
                x[c * group * 32 : (c + 1) * group * 32, :], stacked, preferred_element_type=F32
            ).astype(BF16)
            for i in range(group):
                b = c * group + i
                e1[0:32, b * 128 : (b + 1) * 128] = part[i * 32 : (i + 1) * 32]
            at = pl.ds(c * group * 128, group * 128)
            sends = [
                remote(e1.at[0:16, at], e1.at[48:64, at], dn_s.at[c], dn_r.at[c], (w_me, lower)),
                remote(e1.at[16:32, at], e1.at[32:48, at], up_s.at[c], up_r.at[c], (w_me, upper)),
            ]
            for copy in sends:
                copy.start()
            halo1 += sends
            if c == 0:
                with jax.named_scope("cotangent_stage_2"):
                    for copy in ag1:
                        copy.wait_recv()
                    at0 = pl.ds(pl.multiple_of(z_me * side, side), side)
                    at1 = pl.ds(pl.multiple_of(y_me * side, side), side)
                    for d in steps:
                        ag2.append(
                            remote(g0.at[at0], g0.at[at0], ag2_s.at[0, d - 1], ag2_r.at[0, d - 1], at_z(along_z(d)))
                        )
                        ag2.append(
                            remote(g1.at[at1], g1.at[at1], ag2_s.at[1, d - 1], ag2_r.at[1, d - 1], at_y(along_y(d)))
                        )
                    for copy in ag2:
                        copy.start()

    with jax.named_scope("bands"):
        loads[6].wait()
        first_level = l_me * 8
        top = n_lev * 8
        half = iota((8, width), 0) < 4

        def pairs_of(v):
            r = pltpu.roll(v, 4, 0)
            return jnp.where(half, v, r), jnp.where(half, r, v)

        band_v[...] = jnp.transpose(vloc_v[...])
        lows, highs = pairs_of(band_v[pl.ds(pl.multiple_of(first_level, 8), 8), :])
        _, before = pairs_of(band_v[pl.ds(pl.multiple_of(jnp.maximum(first_level - 8, 0), 8), 8), :])
        after, _ = pairs_of(band_v[pl.ds(pl.multiple_of(jnp.minimum(first_level + 8, top - 8), 8), 8), :])

        def source_level(k):
            g, q = k // 16, k % 4
            return jnp.where(g == 0, q, jnp.where(g == 1, q + 4, jnp.where(g == 2, q - 4, q + 8)))

        def banded(values, inside, offset):
            total = jnp.zeros(offset.shape, F32)
            for o in range(width):
                column = jnp.broadcast_to(values[:, o : o + 1], offset.shape)
                total = total + jnp.where(inside & (offset == o), column, 0.0)
            return total

        def in_two(w):
            top_part = w.astype(BF16)
            rest = (w - top_part.astype(F32)).astype(BF16)
            return jnp.concatenate([top_part, rest], axis=0)

        shape = (32, 64)
        r, k = iota(shape, 0), iota(shape, 1)
        level_out, level_in = (r // 16) * 4 + r % 4, source_level(k)
        inside = ((r % 16) // 4 == (k % 16) // 4) & (first_level + level_in >= 0) & (first_level + level_in < top)
        down = in_two(
            banded(jnp.concatenate([lows, lows, highs, highs], axis=0), inside, level_in - level_out + REACH)
        )
        shape = (128, 128)
        k, r = iota(shape, 0), iota(shape, 1)
        level_out, level_in = r % 8, source_level(k)
        inside = (r // 8 == (k % 16) // 4) & (first_level + level_in >= 0) & (first_level + level_in < top)
        inside = inside & (k < 64) & (r < 32)
        rows_in = [lows, lows, highs, highs, before, before, after, after] + [jnp.zeros((8, width), F32)] * 8
        up = banded(jnp.concatenate(rows_in, axis=0), inside, level_out - level_in + REACH)
        up = in_two(jnp.transpose(up)[0:32, 0:64])

    with jax.named_scope("ensemble"):
        loads[7].wait()

        def split_ens(b, _):
            a = ens_v[0, :, :, block_lanes(b)].astype(F32)
            ens_f[b] = halves_of([a[f] for f in range(4)])
            return 0

        lax.fori_loop(0, blocks, split_ens, 0, unroll=4)
        for k in range(slots):
            tiles_nt[:, k * 128 : (k + 1) * 128] = tile_v[k]

    with jax.named_scope("mix_down"):
        for copy in halo1:
            copy.wait_recv()
        wide_mix = min(4, blocks)

        def down_step(i, _):
            at = pl.ds(pl.multiple_of(i * wide_mix * 128, wide_mix * 128), wide_mix * 128)
            both = jnp.dot(down, e1[:, at], preferred_element_type=F32)
            local = (both[:32] + both[32:]).astype(BF16).astype(F32)
            for j in range(wide_mix):
                b = i * wide_mix + j
                p3[b] = local[:, j * 128 : (j + 1) * 128] * ens_f[b]
            return 0

        lax.fori_loop(0, blocks // wide_mix, down_step, 0, unroll=2)

    with jax.named_scope("member_sum_stage_1"):

        def share(w, _):
            start = tab_s[base, w]
            blk = lax.shift_right_logical(start, 7)
            t = jnp.where(lane32 >= (start & 127), p3[blk], p3[jnp.minimum(blk + 1, blocks - 1)]).astype(BF16)
            h0[w] = t[:16]
            h1[lax.rem(w, side) * side + lax.div(w, side)] = t[16:]
            return 0

        lax.fori_loop(0, n_wide, share, 0, unroll=4)
        rs1 = []
        for d in steps:
            z, y = along_z(d), along_y(d)
            at0 = pl.ds(pl.multiple_of(z * side, side), side)
            at1 = pl.ds(pl.multiple_of(y * side, side), side)
            rs1.append(remote(h0.at[at0], r0.at[d - 1], rs1_s.at[0, d - 1], rs1_r.at[0, d - 1], at_z(z)))
            rs1.append(remote(h1.at[at1], r1.at[d - 1], rs1_s.at[1, d - 1], rs1_r.at[1, d - 1], at_y(y)))
        for copy in rs1:
            copy.start()

    with jax.named_scope("scaled"):
        for copy in ag2:
            copy.wait_recv()

        def paint(r, acc):
            o = tab_s[base + 4, r]
            start, size = tab_s[base + 2, r] & 127, tab_s[base + 3, r]
            tile = jnp.concatenate([g0[o], g1[(o & (side - 1)) * side + lax.div(o, side)]], axis=0).astype(F32)
            acc = jnp.where((lane32 >= start) & (lane32 < start + size), tile, acc)
            snap[r] = acc
            return jnp.where(lane32 < start + size - 128, tile, acc)

        lax.fori_loop(0, n_wide, paint, jnp.zeros((32, 128), F32), unroll=4)
        halo2 = []
        for c in range(n_groups):

            def scale(i, _, c=c):
                b = c * group + i
                e2[0:32, block_lanes(b)] = (ens_f[b] * snap[tab_s[base + 5, b]]).astype(BF16)
                return 0

            lax.fori_loop(0, group, scale, 0, unroll=4)
            at = pl.ds(c * group * 128, group * 128)
            sends = [
                remote(e2.at[0:16, at], e2.at[48:64, at], bdn_s.at[c], bdn_r.at[c], (w_me, lower)),
                remote(e2.at[16:32, at], e2.at[32:48, at], bup_s.at[c], bup_r.at[c], (w_me, upper)),
            ]
            for copy in sends:
                copy.start()
            halo2 += sends

    with jax.named_scope("mix_up"):
        for k in range(slots):
            run[k, blocks] = jnp.zeros((32, 128), F32)
        for copy in halo2:
            copy.wait_recv()

        def up_step(i, _):
            at = pl.ds(pl.multiple_of(i * wide_mix * 128, wide_mix * 128), wide_mix * 128)
            both = jnp.dot(up, e2[:, at], preferred_element_type=F32)
            local = (both[:32] + both[32:]).astype(BF16).astype(F32)
            for j in range(wide_mix):
                mixed[i * wide_mix + j] = local[:, j * 128 : (j + 1) * 128]
            return 0

        lax.fori_loop(0, blocks // wide_mix, up_step, 0, unroll=2)

        def link(b, _):
            m = mixed[b]
            for k in range(slots):
                run[k, b] = m + run[k, tab_s[slots + k, b]]
            return 0

        lax.fori_loop(0, blocks, link, 0)

    with jax.named_scope("gradient"):
        outs = []
        for c in range(n_groups):

            def pick_back(i, _, c=c):
                j = c * group + i
                at = pl.ds(pl.multiple_of(j * 32, 32), 32)
                for k in range(slots):
                    x[at, k * 128 : (k + 1) * 128] = run[k, tab_s[2 * slots + k, j]].astype(BF16)
                return 0

            lax.fori_loop(0, group, pick_back, 0, unroll=2)
            part = lax.dot_general(
                x[c * group * 32 : (c + 1) * group * 32, :],
                tiles_nt[...],
                (((1,), (1,)), ((), ())),
                preferred_element_type=F32,
            )
            for i in range(group):
                for f in range(4):
                    j = c * group + i
                    grad_v[f, :, j * 128 : (j + 1) * 128] = part[i * 32 + f * 8 : i * 32 + f * 8 + 8].astype(BF16)
            at = pl.ds(c * group * 128, group * 128)
            out = pltpu.make_async_copy(grad_v.at[:, :, at], grad_h.at[0, :, :, at], out_sem.at[c])
            out.start()
            outs.append(out)

    with jax.named_scope("member_sum_stage_2"):
        for copy in rs1:
            copy.wait_recv()

        for h, got, q, qf, me in ((h0, r0, q0, q0f, z_me), (h1, r1, q1, q1f, y_me)):

            def add_up(j, _, h=h, got=got, q=q, qf=qf, me=me):
                total = h[me * side + j].astype(F32)
                for d in range(side - 1):
                    total = total + got[d, j].astype(F32)
                qf[j] = total
                q[j] = total.astype(BF16)
                return 0

            lax.fori_loop(0, side, add_up, 0, unroll=2)
        rs2 = []
        for d in steps:
            z, y = along_z(d), along_y(d)
            rs2.append(remote(q0.at[y], t0.at[d - 1], rs2_s.at[0, d - 1], rs2_r.at[0, d - 1], at_y(y)))
            rs2.append(remote(q1.at[z], t1.at[d - 1], rs2_s.at[1, d - 1], rs2_r.at[1, d - 1], at_z(z)))
        for copy in rs2:
            copy.start()
        for copy in rs2:
            copy.wait_recv()
        total0, total1 = q0f[y_me], q1f[z_me]
        for d in range(side - 1):
            total0 = total0 + t0[d].astype(F32)
            total1 = total1 + t1[d].astype(F32)
        total = jnp.concatenate([total0, total1], axis=0) * (1.0 / math.sqrt(members))
        total = pltpu.roll(total, (128 - my_off) & 127, 1)
        total = jnp.where(lane32 < my_size, total, 0.0)
        for f, value in enumerate(fields_of(total)):
            inc_v[f] = value.astype(BF16)
        out = pltpu.make_async_copy(inc_v, inc_h, out_sem.at[n_groups])
        out.start()
        outs.append(out)

    with jax.named_scope("drain"):
        for copy in ag1 + ag2 + rs1 + rs2 + halo1 + halo2:
            copy.wait_send()
        for out in outs:
            out.wait()


def body(n_wide, n_lev, alpha, ens, htile, vloc, pattern, region_sizes, owner, cotangent):
    side = math.isqrt(n_wide)
    columns = alpha.shape[3]
    blocks = columns // 128
    slots = htile.shape[0]
    width = vloc.shape[1]
    group = min(8, blocks)
    n_groups = blocks // group
    dma = pltpu.SemaphoreType.DMA
    vmem = pltpu.VMEM
    ring = side - 1
    scratch = [
        vmem(alpha.shape, BF16), vmem(ens.shape, BF16), vmem(htile.shape, BF16), vmem(vloc.shape[::-1], F32),
        vmem(pattern.shape[::-1], I32), vmem((1, n_wide), I32), vmem((1, n_wide), I32), vmem(cotangent.shape, BF16),
        vmem((32, 128), I32), pltpu.SMEM((32, 128), I32),
        vmem((blocks, 32, 128), BF16),
        vmem((blocks * 32, slots * 128), BF16),
        vmem((128, slots * 128), BF16),
        vmem(vloc.shape, F32),
        vmem((blocks, 32, 128), F32),
        vmem((64, columns), BF16), vmem((64, columns), BF16),
        vmem((blocks, 32, 128), F32),
        vmem((n_wide, 16, 128), BF16), vmem((n_wide, 16, 128), BF16),
        vmem((ring, side, 16, 128), BF16), vmem((ring, side, 16, 128), BF16),
        vmem((side, 16, 128), BF16), vmem((side, 16, 128), BF16),
        vmem((side, 16, 128), F32), vmem((side, 16, 128), F32),
        vmem((ring, 16, 128), BF16), vmem((ring, 16, 128), BF16),
        vmem((n_wide, 16, 128), BF16), vmem((n_wide, 16, 128), BF16),
        vmem((n_wide, 32, 128), F32),
        vmem((blocks, 32, 128), F32),
        vmem((slots, blocks + 1, 32, 128), F32),
        vmem(alpha.shape[1:], BF16), vmem(cotangent.shape, BF16),
        dma((9,)), dma((n_groups + 1,)),
        *[dma((2, ring))] * 8,
        *[dma((n_groups,))] * 8,
    ]
    any_spec = pl.BlockSpec(memory_space=pl.ANY)
    return pl.pallas_call(
        functools.partial(kernel, side, n_lev, blocks, slots, n_wide, width),
        out_shape=(
            jax.ShapeDtypeStruct(cotangent.shape, BF16),
            jax.ShapeDtypeStruct(alpha.shape, BF16),
        ),
        in_specs=[any_spec] * 8,
        out_specs=(any_spec, any_spec),
        scratch_shapes=scratch,
        compiler_params=pltpu.CompilerParams(
            collective_id=0, has_side_effects=True, vmem_limit_bytes=VMEM_LIMIT
        ),
    )(
        alpha, ens, htile, vloc.T, pattern.T,
        region_sizes.reshape(1, n_wide), owner.reshape(1, n_wide), cotangent,
    )


def solution(mesh):
    placed = (
        P("wide", None, "lev", None),
        P("wide", None, "lev", None),
        P(),
        P(),
        P(),
        P(),
        P(),
        P(None, "lev", "wide"),
    )
    return jax.shard_map(
        functools.partial(body, mesh.shape["wide"], mesh.shape["lev"]),
        mesh=mesh,
        in_specs=placed,
        out_specs=(P(None, "lev", "wide"), P("wide", None, "lev", None)),
        check_vma=False,
    )
```

time: 302 us -> 46 us (0.15)
  local copies, waits for them, and re-layouts: 138 us -> 2.96 us
  other arithmetic: 89.8 us -> 0 us
  Pallas kernels: 0 us -> 42.2 us
  starting transfers between devices: 40.1 us -> 0 us
  waiting for transfers between devices: 24.8 us -> 0 us
  matrix products: 5.61 us -> 0 us
    gather x14 -> x0, local copies, waits for them, and re-layouts: 120 us -> none  [the longest x2 75.2 us: body(): jnp.take(partial_value, source, axis=2) * valid_slot.astype(jnp.float32)]
    and x2 -> x0, other arithmetic: 71.4 us -> none  [the longest x1 71.3 us: body(): cot_cols = jnp.take(gathered, slot_of, axis=2)]
    pallas_call x0 -> x1, Pallas kernels: none -> 42.2 us  [body(): pl.pallas_call(functools.partial(kernel, side, n_lev, blocks, slots, n_wi...]
    all_to_all x2 -> x0, starting transfers between devices: 24.8 us -> none  [the longest x1 12.5 us: sent_and_summed(): lax.all_to_all(in_blocks(array, dim, peers), axis, 0, 0, tiled=True)]
    all_to_all x2 -> x0, waiting for transfers between devices: 24.8 us -> none  [the longest x1 24.8 us: sent_and_summed(): lax.all_to_all(in_blocks(array, dim, peers), axis, 0, 0, tiled=True)]
    ppermute x4 -> x0, starting transfers between devices: 15.3 us -> none  [the longest x2 10.7 us: padded_2(): lax.ppermute(lax.slice_in_dim(block, 0, width, axis=dim), axis, backward)]
    gather x6 -> x0, other arithmetic: 11.8 us -> none  [the longest x2 7.41 us: slot_tables(): owner[region_of] * region_max + column_ids - region_starts[region_of]]
    reshape x1 -> x0, local copies, waits for them, and re-layouts: 8.12 us -> none  [joined_along(): return jnp.moveaxis(blocks, 0, dim).reshape(shape)]
  transfers between devices with their start and end apart: 6 -> 0, of which waited for: 1 -> 0; matrix products, arithmetic and copies ran while one was open for 61% -> 0% of each run, Pallas kernels for 0% -> 0%
where the time goes in v1:
time: 46 us; the launch traced here: 45.8 us
  Pallas kernels  42.2 us (92%)
  local copies, waits for them, and re-layouts  2.96 us (6%)
  between operations  0.64 us (1%)
    pallas_call x1, Pallas kernels, body(): pl.pallas_call(functools.partial(kernel, side, n_lev, blocks, slots, n_wi...  42.2 us
    unnamed x2, local copies, waits for them, and re-layouts  2.96 us

profile of v1, /device:TPU:1, one launch (start us, length us, event | category | flops | bytes accessed | tf_op | source)
XLA Modules:
  0.0 45.8 jit_solution(10670910239046636975)
XLA Ops:
  0.6 42.2 %shard_map.95 = (bf16[4,8,128]{2,1,0:T(8,128)(2,1)}, bf16[1,4,8,4096]{3,2,1,0:T(8,128)(2,1)}) custom-call(bf16[1,4,8,4096]{3,2,1,0:T(8,128)(2,1)} %alpha_h.1, bf16[1,4,8,4096]{3,2,1,0:T(8,128)(2,1)} %ens_h.1, bf16[8,128,128]{2,1,0:T(8,128)(2,1)} %htile_h.1, f32[9,64]{1,0:T(8,128)} %bitcast.4, s32[8,32]{1,0:T(8,128)} %bitcast.5, s32[1,64]{1,0:T(1,128)} %bitcast.6, ...), custom_call_target="tpu_custom_call" | custom-call | tf_op jit(solution)/shard_map/pallas_call | solution.py:464
  42.8 1.3 %copy.12 = bf16[4,8,128]{2,1,0:T(8,128)(2,1)} copy(bf16[4,8,128]{2,1,0:T(8,128)(2,1)} %get-tuple-element.4) | data formatting | bytes 16384
  44.1 1.7 %copy.13 = bf16[1,4,8,4096]{3,2,1,0:T(8,128)(2,1)} copy(bf16[1,4,8,4096]{3,2,1,0:T(8,128)(2,1)} %get-tuple-element.5) | data formatting | bytes 524288

commit v2 on v1

--- a/solution.py
+++ b/solution.py
@@ -13,6 +13,7 @@
 F32 = jnp.float32
 BF16 = jnp.bfloat16
 I32 = jnp.int32
+GATHER_AFTER = 1
 VMEM_LIMIT = 60 * 1024 * 1024
 
 
@@ -29,23 +30,12 @@
     return jnp.concatenate(low + high, axis=0)
 
 
-def fields_of(rows):
-    fields = []
-    for pair in range(2):
-        low = rows[8 * pair : 8 * pair + 8]
-        high = rows[16 + 8 * pair : 24 + 8 * pair]
-        first = iota(low.shape, 0) < 4
-        fields.append(jnp.where(first, low, pltpu.roll(high, 4, 0)))
-        fields.append(jnp.where(first, pltpu.roll(low, 4, 0), high))
-    return fields
-
-
 def kernel(
     side, n_lev, blocks, slots, members, width,
     alpha_h, ens_h, htile_h, vloc_h, pattern_h, sizes_h, owner_h, cot_h,
     inc_h, grad_h,
-    alpha_v, ens_v, tile_v, vloc_v, pat_v, size_v, own_v, cot_v, tab_v, tab_s,
-    a3, x, tiles_nt, band_v, ens_f, e1, e2, p3, h0, h1, r0, r1, q0, q1, q0f, q1f, t0, t1,
+    alpha_v, ens_v, tile_v, vloc_v, pat_v, size_v, own_v, tab_v, tab_s,
+    a3, x, tiles_nt, band_v, e1, e2, p3, h0, h1, r0, r1, q0, q1, q0f, q1f, t0, t1,
     g0, g1, snap, mixed, run, grad_v, inc_v,
     local_sem, out_sem, ag1_s, ag1_r, ag2_s, ag2_r, rs1_s, rs1_r, rs2_s, rs2_r, up_s, up_r, dn_s, dn_r,
     bup_s, bup_r, bdn_s, bdn_r,
@@ -54,7 +44,7 @@
     w_me, l_me = lax.axis_index("wide"), lax.axis_index("lev")
     z_me, y_me = w_me // side, w_me % side
     upper, lower = lax.rem(l_me + 1, n_lev), lax.rem(l_me + n_lev - 1, n_lev)
-    steps = range(1, side)
+    steps = sorted(range(1, side), key=lambda d: -min(d, side - d))
 
     def along_y(d):
         return lax.rem(y_me + d, side)
@@ -78,7 +68,7 @@
             pltpu.make_async_copy(src, dst, local_sem.at[i])
             for i, (src, dst) in enumerate(
                 (
-                    (sizes_h, size_v), (owner_h, own_v), (pattern_h, pat_v), (cot_h, cot_v),
+                    (sizes_h, size_v), (owner_h, own_v), (pattern_h, pat_v),
                     (alpha_h, alpha_v), (htile_h, tile_v), (vloc_h, vloc_v), (ens_h, ens_v),
                 )
             )
@@ -91,8 +81,27 @@
         for friend in friends:
             pl.semaphore_signal(barrier, inc=1, device_id=friend, device_id_type=MESH)
 
+    with jax.named_scope("cotangent_stage_1"):
+        own0 = pltpu.make_async_copy(cot_h.at[0:2], g0.at[w_me], local_sem.at[8])
+        own1 = pltpu.make_async_copy(cot_h.at[2:4], g1.at[y_me * side + z_me], local_sem.at[9])
+        own0.start()
+        own1.start()
+        pl.semaphore_wait(barrier, len(friends))
+        ag1 = []
+        for d in steps:
+            ag1.append(
+                remote(cot_h.at[0:2], g0.at[w_me], ag1_s.at[0, d - 1], ag1_r.at[0, d - 1], at_y(along_y(d)))
+            )
+            ag1.append(
+                remote(
+                    cot_h.at[2:4], g1.at[y_me * side + z_me], ag1_s.at[1, d - 1], ag1_r.at[1, d - 1], at_z(along_z(d))
+                )
+            )
+        for copy in ag1:
+            copy.start()
+
     with jax.named_scope("tables"):
-        for load in loads[:4]:
+        for load in loads[:3]:
             load.wait()
         square = (n_wide, n_wide)
         rows, cols = iota(square, 0), iota(square, 1)
@@ -120,35 +129,20 @@
             tab_v[slots + k : slots + k + 1, 0:blocks] = jnp.where(before < 0, blocks, before)
             last = jnp.max(jnp.where(col == there, here, -1), axis=0, keepdims=True)
             tab_v[2 * slots + k : 2 * slots + k + 1, 0:blocks] = jnp.where(last < 0, blocks, last)
-        to_s = pltpu.make_async_copy(tab_v, tab_s, local_sem.at[8])
+        to_s = pltpu.make_async_copy(tab_v, tab_s, local_sem.at[7])
         to_s.start()
         to_s.wait()
         my_start = tab_s[base, w_me]
         my_size = tab_s[base + 1, w_me]
         my_off = my_start & 127
 
-    lane16 = iota((16, 128), 1)
     lane32 = iota((32, 128), 1)
-
-    with jax.named_scope("cotangent_stage_1"):
-        cot = cot_v[...].astype(F32)
-        tile = pltpu.roll(halves_of([cot[f] for f in range(4)]), my_off, 1)
-        g0[w_me] = tile[:16].astype(BF16)
-        g1[y_me * side + z_me] = tile[16:].astype(BF16)
-        pl.semaphore_wait(barrier, len(friends))
-        i0, i1 = w_me, y_me * side + z_me
-        ag1 = []
-        for d in steps:
-            ag1.append(remote(g0.at[i0], g0.at[i0], ag1_s.at[0, d - 1], ag1_r.at[0, d - 1], at_y(along_y(d))))
-            ag1.append(remote(g1.at[i1], g1.at[i1], ag1_s.at[1, d - 1], ag1_r.at[1, d - 1], at_z(along_z(d))))
-        for copy in ag1:
-            copy.start()
 
     def block_lanes(b):
         return pl.ds(pl.multiple_of(b * 128, 128), 128)
 
     with jax.named_scope("spread"):
-        loads[4].wait()
+        loads[3].wait()
 
         def split_alpha(b, _):
             a = alpha_v[0, :, :, block_lanes(b)].astype(F32)
@@ -156,7 +150,7 @@
             return 0
 
         lax.fori_loop(0, blocks, split_alpha, 0, unroll=4)
-        loads[5].wait()
+        loads[4].wait()
         stacked = tile_v[...].reshape(slots * 128, 128)
         group = min(8, blocks)
         n_groups = blocks // group
@@ -186,10 +180,12 @@
             for copy in sends:
                 copy.start()
             halo1 += sends
-            if c == 0:
+            if c == min(GATHER_AFTER, n_groups - 1):
                 with jax.named_scope("cotangent_stage_2"):
                     for copy in ag1:
                         copy.wait_recv()
+                    own0.wait()
+                    own1.wait()
                     at0 = pl.ds(pl.multiple_of(z_me * side, side), side)
                     at1 = pl.ds(pl.multiple_of(y_me * side, side), side)
                     for d in steps:
@@ -203,7 +199,7 @@
                         copy.start()
 
     with jax.named_scope("bands"):
-        loads[6].wait()
+        loads[5].wait()
         first_level = l_me * 8
         top = n_lev * 8
         half = iota((8, width), 0) < 4
@@ -213,7 +209,8 @@
             return jnp.where(half, v, r), jnp.where(half, r, v)
 
         band_v[...] = jnp.transpose(vloc_v[...])
-        lows, highs = pairs_of(band_v[pl.ds(pl.multiple_of(first_level, 8), 8), :])
+        band = band_v[pl.ds(pl.multiple_of(first_level, 8), 8), :]
+        lows, highs = pairs_of(band)
         _, before = pairs_of(band_v[pl.ds(pl.multiple_of(jnp.maximum(first_level - 8, 0), 8), 8), :])
         after, _ = pairs_of(band_v[pl.ds(pl.multiple_of(jnp.minimum(first_level + 8, top - 8), 8), 8), :])
 
@@ -235,11 +232,9 @@
 
         shape = (32, 64)
         r, k = iota(shape, 0), iota(shape, 1)
-        level_out, level_in = (r // 16) * 4 + r % 4, source_level(k)
-        inside = ((r % 16) // 4 == (k % 16) // 4) & (first_level + level_in >= 0) & (first_level + level_in < top)
-        down = in_two(
-            banded(jnp.concatenate([lows, lows, highs, highs], axis=0), inside, level_in - level_out + REACH)
-        )
+        level_out, level_in = r % 8, source_level(k)
+        inside = (r // 8 == (k % 16) // 4) & (first_level + level_in >= 0) & (first_level + level_in < top)
+        down = in_two(banded(jnp.concatenate([band] * 4, axis=0), inside, level_in - level_out + REACH))
         shape = (128, 128)
         k, r = iota(shape, 0), iota(shape, 1)
         level_out, level_in = r % 8, source_level(k)
@@ -250,21 +245,17 @@
         up = in_two(jnp.transpose(up)[0:32, 0:64])
 
     with jax.named_scope("ensemble"):
-        loads[7].wait()
-
-        def split_ens(b, _):
-            a = ens_v[0, :, :, block_lanes(b)].astype(F32)
-            ens_f[b] = halves_of([a[f] for f in range(4)])
-            return 0
-
-        lax.fori_loop(0, blocks, split_ens, 0, unroll=4)
+        loads[6].wait()
+
+        def ens_block(b):
+            return ens_v[0, :, :, block_lanes(b)].astype(F32).reshape(32, 128)
+
         for k in range(slots):
             tiles_nt[:, k * 128 : (k + 1) * 128] = tile_v[k]
 
     with jax.named_scope("mix_down"):
-        for copy in halo1:
-            copy.wait_recv()
         wide_mix = min(4, blocks)
+        mixes = group // wide_mix
 
         def down_step(i, _):
             at = pl.ds(pl.multiple_of(i * wide_mix * 128, wide_mix * 128), wide_mix * 128)
@@ -272,10 +263,13 @@
             local = (both[:32] + both[32:]).astype(BF16).astype(F32)
             for j in range(wide_mix):
                 b = i * wide_mix + j
-                p3[b] = local[:, j * 128 : (j + 1) * 128] * ens_f[b]
+                p3[b] = local[:, j * 128 : (j + 1) * 128] * ens_block(b)
             return 0
 
-        lax.fori_loop(0, blocks // wide_mix, down_step, 0, unroll=2)
+        for c in range(n_groups):
+            for copy in halo1[2 * c : 2 * c + 2]:
+                copy.wait_recv()
+            lax.fori_loop(c * mixes, (c + 1) * mixes, down_step, 0, unroll=mixes)
 
     with jax.named_scope("member_sum_stage_1"):
 
@@ -305,7 +299,9 @@
         def paint(r, acc):
             o = tab_s[base + 4, r]
             start, size = tab_s[base + 2, r] & 127, tab_s[base + 3, r]
-            tile = jnp.concatenate([g0[o], g1[(o & (side - 1)) * side + lax.div(o, side)]], axis=0).astype(F32)
+            first = g0[o].astype(F32).reshape(16, 128)
+            second = g1[(o & (side - 1)) * side + lax.div(o, side)].astype(F32).reshape(16, 128)
+            tile = pltpu.roll(jnp.concatenate([first, second], axis=0), start, 1)
             acc = jnp.where((lane32 >= start) & (lane32 < start + size), tile, acc)
             snap[r] = acc
             return jnp.where(lane32 < start + size - 128, tile, acc)
@@ -316,7 +312,8 @@
 
             def scale(i, _, c=c):
                 b = c * group + i
-                e2[0:32, block_lanes(b)] = (ens_f[b] * snap[tab_s[base + 5, b]]).astype(BF16)
+                s = ens_block(b) * snap[tab_s[base + 5, b]]
+                e2[0:32, block_lanes(b)] = halves_of([s[8 * f : 8 * f + 8] for f in range(4)]).astype(BF16)
                 return 0
 
             lax.fori_loop(0, group, scale, 0, unroll=4)
@@ -332,9 +329,6 @@
     with jax.named_scope("mix_up"):
         for k in range(slots):
             run[k, blocks] = jnp.zeros((32, 128), F32)
-        for copy in halo2:
-            copy.wait_recv()
-
         def up_step(i, _):
             at = pl.ds(pl.multiple_of(i * wide_mix * 128, wide_mix * 128), wide_mix * 128)
             both = jnp.dot(up, e2[:, at], preferred_element_type=F32)
@@ -343,15 +337,42 @@
                 mixed[i * wide_mix + j] = local[:, j * 128 : (j + 1) * 128]
             return 0
 
-        lax.fori_loop(0, blocks // wide_mix, up_step, 0, unroll=2)
+        for c in range(n_groups):
+            for copy in halo2[2 * c : 2 * c + 2]:
+                copy.wait_recv()
+            lax.fori_loop(c * mixes, (c + 1) * mixes, up_step, 0, unroll=mixes)
 
         def link(b, _):
             m = mixed[b]
+            earlier = [run[k, tab_s[slots + k, b]] for k in range(slots)]
             for k in range(slots):
-                run[k, b] = m + run[k, tab_s[slots + k, b]]
+                run[k, b] = m + earlier[k]
             return 0
 
         lax.fori_loop(0, blocks, link, 0)
+
+    with jax.named_scope("member_sum_stage_2"):
+        for copy in rs1:
+            copy.wait_recv()
+
+        for h, got, q, qf, me in ((h0, r0, q0, q0f, z_me), (h1, r1, q1, q1f, y_me)):
+
+            def add_up(j, _, h=h, got=got, q=q, qf=qf, me=me):
+                total = h[me * side + j].astype(F32)
+                for d in range(side - 1):
+                    total = total + got[d, j].astype(F32)
+                qf[j] = total
+                q[j] = total.astype(BF16)
+                return 0
+
+            lax.fori_loop(0, side, add_up, 0, unroll=2)
+        rs2 = []
+        for d in steps:
+            z, y = along_z(d), along_y(d)
+            rs2.append(remote(q0.at[y], t0.at[d - 1], rs2_s.at[0, d - 1], rs2_r.at[0, d - 1], at_y(y)))
+            rs2.append(remote(q1.at[z], t1.at[d - 1], rs2_s.at[1, d - 1], rs2_r.at[1, d - 1], at_z(z)))
+        for copy in rs2:
+            copy.start()
 
     with jax.named_scope("gradient"):
         outs = []
@@ -380,28 +401,7 @@
             out.start()
             outs.append(out)
 
-    with jax.named_scope("member_sum_stage_2"):
-        for copy in rs1:
-            copy.wait_recv()
-
-        for h, got, q, qf, me in ((h0, r0, q0, q0f, z_me), (h1, r1, q1, q1f, y_me)):
-
-            def add_up(j, _, h=h, got=got, q=q, qf=qf, me=me):
-                total = h[me * side + j].astype(F32)
-                for d in range(side - 1):
-                    total = total + got[d, j].astype(F32)
-                qf[j] = total
-                q[j] = total.astype(BF16)
-                return 0
-
-            lax.fori_loop(0, side, add_up, 0, unroll=2)
-        rs2 = []
-        for d in steps:
-            z, y = along_z(d), along_y(d)
-            rs2.append(remote(q0.at[y], t0.at[d - 1], rs2_s.at[0, d - 1], rs2_r.at[0, d - 1], at_y(y)))
-            rs2.append(remote(q1.at[z], t1.at[d - 1], rs2_s.at[1, d - 1], rs2_r.at[1, d - 1], at_z(z)))
-        for copy in rs2:
-            copy.start()
+    with jax.named_scope("increment"):
         for copy in rs2:
             copy.wait_recv()
         total0, total1 = q0f[y_me], q1f[z_me]
@@ -411,8 +411,8 @@
         total = jnp.concatenate([total0, total1], axis=0) * (1.0 / math.sqrt(members))
         total = pltpu.roll(total, (128 - my_off) & 127, 1)
         total = jnp.where(lane32 < my_size, total, 0.0)
-        for f, value in enumerate(fields_of(total)):
-            inc_v[f] = value.astype(BF16)
+        for f in range(4):
+            inc_v[f] = total[8 * f : 8 * f + 8].astype(BF16)
         out = pltpu.make_async_copy(inc_v, inc_h, out_sem.at[n_groups])
         out.start()
         outs.append(out)
@@ -422,6 +422,15 @@
             copy.wait_send()
         for out in outs:
             out.wait()
+
+
+def hand_over(inc_h, grad_h, inc_out, grad_out, sem):
+    copies = [pltpu.make_async_copy(inc_h, inc_out, sem.at[0])]
+    copies += [pltpu.make_async_copy(grad_h.at[0, f], grad_out.at[0, f], sem.at[1 + f]) for f in range(4)]
+    for copy in copies:
+        copy.start()
+    for copy in copies:
+        copy.wait()
 
 
 def body(n_wide, n_lev, alpha, ens, htile, vloc, pattern, region_sizes, owner, cotangent):
@@ -437,13 +446,12 @@
     ring = side - 1
     scratch = [
         vmem(alpha.shape, BF16), vmem(ens.shape, BF16), vmem(htile.shape, BF16), vmem(vloc.shape[::-1], F32),
-        vmem(pattern.shape[::-1], I32), vmem((1, n_wide), I32), vmem((1, n_wide), I32), vmem(cotangent.shape, BF16),
+        vmem(pattern.shape[::-1], I32), vmem((1, n_wide), I32), vmem((1, n_wide), I32),
         vmem((32, 128), I32), pltpu.SMEM((32, 128), I32),
         vmem((blocks, 32, 128), BF16),
         vmem((blocks * 32, slots * 128), BF16),
         vmem((128, slots * 128), BF16),
         vmem(vloc.shape, F32),
-        vmem((blocks, 32, 128), F32),
         vmem((64, columns), BF16), vmem((64, columns), BF16),
         vmem((blocks, 32, 128), F32),
         vmem((n_wide, 16, 128), BF16), vmem((n_wide, 16, 128), BF16),
@@ -451,22 +459,20 @@
         vmem((side, 16, 128), BF16), vmem((side, 16, 128), BF16),
         vmem((side, 16, 128), F32), vmem((side, 16, 128), F32),
         vmem((ring, 16, 128), BF16), vmem((ring, 16, 128), BF16),
-        vmem((n_wide, 16, 128), BF16), vmem((n_wide, 16, 128), BF16),
+        vmem((n_wide, 2, 8, 128), BF16), vmem((n_wide, 2, 8, 128), BF16),
         vmem((n_wide, 32, 128), F32),
         vmem((blocks, 32, 128), F32),
         vmem((slots, blocks + 1, 32, 128), F32),
         vmem(alpha.shape[1:], BF16), vmem(cotangent.shape, BF16),
-        dma((9,)), dma((n_groups + 1,)),
+        dma((10,)), dma((n_groups + 1,)),
         *[dma((2, ring))] * 8,
         *[dma((n_groups,))] * 8,
     ]
     any_spec = pl.BlockSpec(memory_space=pl.ANY)
-    return pl.pallas_call(
+    shapes = (jax.ShapeDtypeStruct(cotangent.shape, BF16), jax.ShapeDtypeStruct(alpha.shape, BF16))
+    results = pl.pallas_call(
         functools.partial(kernel, side, n_lev, blocks, slots, n_wide, width),
-        out_shape=(
-            jax.ShapeDtypeStruct(cotangent.shape, BF16),
-            jax.ShapeDtypeStruct(alpha.shape, BF16),
-        ),
+        out_shape=shapes,
         in_specs=[any_spec] * 8,
         out_specs=(any_spec, any_spec),
         scratch_shapes=scratch,
@@ -477,6 +483,7 @@
         alpha, ens, htile, vloc.T, pattern.T,
         region_sizes.reshape(1, n_wide), owner.reshape(1, n_wide), cotangent,
     )
+    return results
 
 
 def solution(mesh):

time: 46 us -> 44 us (0.957); the launches traced: 45.8 us -> 43.2 us
  Pallas kernels: 42.2 us -> 39.6 us
    pallas_call x1, Pallas kernels: 42.2 us -> 39.6 us  [body(): pl.pallas_call(functools.partial(kernel, side, n_lev, blocks, slots, n_wi...]
where the time goes in v2:
time: 44 us; the launch traced here: 43.2 us
  Pallas kernels  39.6 us (90%)
  local copies, waits for them, and re-layouts  2.96 us (7%)
  between operations  0.64 us (1%)
    pallas_call x1, Pallas kernels, body(): pl.pallas_call(functools.partial(kernel, side, n_lev, blocks, slots, n_wi...  39.6 us
    unnamed x2, local copies, waits for them, and re-layouts  2.96 us

profile of v2, /device:TPU:1, one launch (start us, length us, event | category | flops | bytes accessed | tf_op | source)
XLA Modules:
  0.0 43.2 jit_solution(17114950683055961956)
XLA Ops:
  0.6 39.6 %shard_map.95 = (bf16[4,8,128]{2,1,0:T(8,128)(2,1)}, bf16[1,4,8,4096]{3,2,1,0:T(8,128)(2,1)}) custom-call(bf16[1,4,8,4096]{3,2,1,0:T(8,128)(2,1)} %alpha_h.1, bf16[1,4,8,4096]{3,2,1,0:T(8,128)(2,1)} %ens_h.1, bf16[8,128,128]{2,1,0:T(8,128)(2,1)} %htile_h.1, f32[9,64]{1,0:T(8,128)} %bitcast.4, s32[8,32]{1,0:T(8,128)} %bitcast.5, s32[1,64]{1,0:T(1,128)} %bitcast.6, ...), custom_call_target="tpu_custom_call" | custom-call | tf_op jit(solution)/shard_map/pallas_call | solution.py:473
  40.2 1.3 %copy.12 = bf16[4,8,128]{2,1,0:T(8,128)(2,1)} copy(bf16[4,8,128]{2,1,0:T(8,128)(2,1)} %get-tuple-element.4) | data formatting | bytes 16384
  41.5 1.7 %copy.13 = bf16[1,4,8,4096]{3,2,1,0:T(8,128)(2,1)} copy(bf16[1,4,8,4096]{3,2,1,0:T(8,128)(2,1)} %get-tuple-element.5) | data formatting | bytes 524288

commit v3 on v2

--- a/solution.py
+++ b/solution.py
@@ -36,15 +36,20 @@
     inc_h, grad_h,
     alpha_v, ens_v, tile_v, vloc_v, pat_v, size_v, own_v, tab_v, tab_s,
     a3, x, tiles_nt, band_v, e1, e2, p3, h0, h1, r0, r1, q0, q1, q0f, q1f, t0, t1,
-    g0, g1, snap, mixed, run, grad_v, inc_v,
+    g0, g1, snap, run, grad_v, inc_v,
     local_sem, out_sem, ag1_s, ag1_r, ag2_s, ag2_r, rs1_s, rs1_r, rs2_s, rs2_r, up_s, up_r, dn_s, dn_r,
     bup_s, bup_r, bdn_s, bdn_r,
 ):
     n_wide = side * side
+    bits = side.bit_length() - 1
     w_me, l_me = lax.axis_index("wide"), lax.axis_index("lev")
     z_me, y_me = w_me // side, w_me % side
     upper, lower = lax.rem(l_me + 1, n_lev), lax.rem(l_me + n_lev - 1, n_lev)
     steps = sorted(range(1, side), key=lambda d: -min(d, side - d))
+    order = sorted(range(side), key=lambda d: (min(d, side - d), d))
+    place = {d: p for p, d in enumerate(order)}
+    cuts = (0, 1, min(5, side), side)
+    groups = [(g, a, b) for g, (a, b) in enumerate(zip(cuts, cuts[1:])) if a < b]
 
     def along_y(d):
         return lax.rem(y_me + d, side)
@@ -82,23 +87,45 @@
             pl.semaphore_signal(barrier, inc=1, device_id=friend, device_id_type=MESH)
 
     with jax.named_scope("cotangent_stage_1"):
-        own0 = pltpu.make_async_copy(cot_h.at[0:2], g0.at[w_me], local_sem.at[8])
-        own1 = pltpu.make_async_copy(cot_h.at[2:4], g1.at[y_me * side + z_me], local_sem.at[9])
+        own0 = pltpu.make_async_copy(cot_h.at[0:2], g0.at[z_me * side], local_sem.at[8])
+        own1 = pltpu.make_async_copy(cot_h.at[2:4], g1.at[y_me * side], local_sem.at[9])
         own0.start()
         own1.start()
         pl.semaphore_wait(barrier, len(friends))
-        ag1 = []
+        ag1, ag2 = {}, []
         for d in steps:
-            ag1.append(
-                remote(cot_h.at[0:2], g0.at[w_me], ag1_s.at[0, d - 1], ag1_r.at[0, d - 1], at_y(along_y(d)))
+            p = place[side - d]
+            to0, to1 = g0.at[z_me * side + p], g1.at[y_me * side + p]
+            ag1[p] = (
+                remote(cot_h.at[0:2], to0, ag1_s.at[0, d - 1], ag1_r.at[0, d - 1], at_y(along_y(d))),
+                remote(cot_h.at[2:4], to1, ag1_s.at[1, d - 1], ag1_r.at[1, d - 1], at_z(along_z(d))),
             )
-            ag1.append(
-                remote(
-                    cot_h.at[2:4], g1.at[y_me * side + z_me], ag1_s.at[1, d - 1], ag1_r.at[1, d - 1], at_z(along_z(d))
+            for copy in ag1[p]:
+                copy.start()
+
+        def forward(g, a, b):
+            for p in range(max(a, 1), b):
+                for copy in ag1[p]:
+                    copy.wait_recv()
+            at0, at1 = pl.ds(z_me * side + a, b - a), pl.ds(y_me * side + a, b - a)
+            for d in steps:
+                pair = (
+                    remote(
+                        cot_h.at[0:2] if g == 0 else g0.at[at0],
+                        g0.at[z_me * side] if g == 0 else g0.at[at0],
+                        ag2_s.at[0, g, d - 1], ag2_r.at[0, g, d - 1], at_z(along_z(d)),
+                    ),
+                    remote(
+                        cot_h.at[2:4] if g == 0 else g1.at[at1],
+                        g1.at[y_me * side] if g == 0 else g1.at[at1],
+                        ag2_s.at[1, g, d - 1], ag2_r.at[1, g, d - 1], at_y(along_y(d)),
+                    ),
                 )
-            )
-        for copy in ag1:
-            copy.start()
+                for copy in pair:
+                    copy.start()
+                ag2.extend(pair)
+
+        forward(*groups[0])
 
     with jax.named_scope("tables"):
         for load in loads[:3]:
@@ -116,7 +143,14 @@
         tab_v[base + 1 : base + 2, 0:n_wide] = jnp.sum(jnp.where(held, size_c, 0), axis=0, keepdims=True)
         tab_v[base + 2 : base + 3, 0:n_wide] = jnp.sum(jnp.where(cols == rows, start_c, 0), axis=0, keepdims=True)
         tab_v[base + 3 : base + 4, 0:n_wide] = size_v[...]
-        tab_v[base + 4 : base + 5, 0:n_wide] = own_v[...]
+
+
+        def near(d):
+            return jnp.where(2 * d <= side, jnp.maximum(2 * d - 1, 0), 2 * (side - d))
+
+        z_own, y_own = lax.shift_right_logical(own_v[...], bits), own_v[...] & (side - 1)
+        tab_v[base + 4 : base + 5, 0:n_wide] = z_own * side + near((y_own - y_me) & (side - 1))
+        tab_v[base + 6 : base + 7, 0:n_wide] = y_own * side + near((z_own - z_me) & (side - 1))
         ends = iota((n_wide, blocks), 1) * 128 + 127
         covered = jnp.sum(jnp.where(start_c + size_c <= ends, 1, 0), axis=0, keepdims=True)
         tab_v[base + 5 : base + 6, 0:blocks] = jnp.minimum(covered, n_wide - 1)
@@ -136,7 +170,7 @@
         my_size = tab_s[base + 1, w_me]
         my_off = my_start & 127
 
-    lane32 = iota((32, 128), 1)
+    lane16, lane32 = iota((16, 128), 1), iota((32, 128), 1)
 
     def block_lanes(b):
         return pl.ds(pl.multiple_of(b * 128, 128), 128)
@@ -149,13 +183,12 @@
             a3[b] = halves_of([a[f] for f in range(4)]).astype(BF16)
             return 0
 
-        lax.fori_loop(0, blocks, split_alpha, 0, unroll=4)
+        lax.fori_loop(0, blocks, split_alpha, 0, unroll=8)
         loads[4].wait()
         stacked = tile_v[...].reshape(slots * 128, 128)
         group = min(8, blocks)
         n_groups = blocks // group
         halo1 = []
-        ag2 = []
         for c in range(n_groups):
 
             def pick(i, _, c=c):
@@ -165,7 +198,7 @@
                     x[at, k * 128 : (k + 1) * 128] = a3[tab_s[k, b]]
                 return 0
 
-            lax.fori_loop(0, group, pick, 0, unroll=2)
+            lax.fori_loop(0, group, pick, 0, unroll=8)
             part = jnp.dot(
                 x[c * group * 32 : (c + 1) * group * 32, :], stacked, preferred_element_type=F32
             ).astype(BF16)
@@ -181,22 +214,8 @@
                 copy.start()
             halo1 += sends
             if c == min(GATHER_AFTER, n_groups - 1):
-                with jax.named_scope("cotangent_stage_2"):
-                    for copy in ag1:
-                        copy.wait_recv()
-                    own0.wait()
-                    own1.wait()
-                    at0 = pl.ds(pl.multiple_of(z_me * side, side), side)
-                    at1 = pl.ds(pl.multiple_of(y_me * side, side), side)
-                    for d in steps:
-                        ag2.append(
-                            remote(g0.at[at0], g0.at[at0], ag2_s.at[0, d - 1], ag2_r.at[0, d - 1], at_z(along_z(d)))
-                        )
-                        ag2.append(
-                            remote(g1.at[at1], g1.at[at1], ag2_s.at[1, d - 1], ag2_r.at[1, d - 1], at_y(along_y(d)))
-                        )
-                    for copy in ag2:
-                        copy.start()
+                for group_of in groups[1:2]:
+                    forward(*group_of)
 
     with jax.named_scope("bands"):
         loads[5].wait()
@@ -243,6 +262,8 @@
         rows_in = [lows, lows, highs, highs, before, before, after, after] + [jnp.zeros((8, width), F32)] * 8
         up = banded(jnp.concatenate(rows_in, axis=0), inside, level_out - level_in + REACH)
         up = in_two(jnp.transpose(up)[0:32, 0:64])
+        for group_of in groups[2:]:
+            forward(*group_of)
 
     with jax.named_scope("ensemble"):
         loads[6].wait()
@@ -273,50 +294,113 @@
 
     with jax.named_scope("member_sum_stage_1"):
 
-        def share(w, _):
+        def share(w, rows):
             start = tab_s[base, w]
             blk = lax.shift_right_logical(start, 7)
-            t = jnp.where(lane32 >= (start & 127), p3[blk], p3[jnp.minimum(blk + 1, blocks - 1)]).astype(BF16)
-            h0[w] = t[:16]
-            h1[lax.rem(w, side) * side + lax.div(w, side)] = t[16:]
-            return 0
-
-        lax.fori_loop(0, n_wide, share, 0, unroll=4)
-        rs1 = []
-        for d in steps:
-            z, y = along_z(d), along_y(d)
-            at0 = pl.ds(pl.multiple_of(z * side, side), side)
-            at1 = pl.ds(pl.multiple_of(y * side, side), side)
-            rs1.append(remote(h0.at[at0], r0.at[d - 1], rs1_s.at[0, d - 1], rs1_r.at[0, d - 1], at_z(z)))
-            rs1.append(remote(h1.at[at1], r1.at[d - 1], rs1_s.at[1, d - 1], rs1_r.at[1, d - 1], at_y(y)))
-        for copy in rs1:
-            copy.start()
+            first, second = p3[blk, rows], p3[jnp.minimum(blk + 1, blocks - 1), rows]
+            return jnp.where(lane16 >= (start & 127), first, second).astype(BF16)
+
+        rs1 = {}
+        for g, a, b in reversed(groups):
+
+            def shares(i, _, a=a, b=b):
+                for p in range(a, b):
+                    h0[i * side + p] = share(i * side + along_y(order[p]), slice(0, 16))
+                    h1[i * side + p] = share(along_z(order[p]) * side + i, slice(16, 32))
+                return 0
+
+            lax.fori_loop(0, side, shares, 0, unroll=2)
+            rs1[g] = []
+            for d in steps:
+                z, y = along_z(d), along_y(d)
+                at0, at1, to = pl.ds(z * side + a, b - a), pl.ds(y * side + a, b - a), pl.ds(a, b - a)
+                rs1[g].append(
+                    remote(h0.at[at0], r0.at[d - 1, to], rs1_s.at[0, g, d - 1], rs1_r.at[0, g, d - 1], at_z(z))
+                )
+                rs1[g].append(
+                    remote(h1.at[at1], r1.at[d - 1, to], rs1_s.at[1, g, d - 1], rs1_r.at[1, g, d - 1], at_y(y))
+                )
+            for copy in rs1[g]:
+                copy.start()
+
+        rs2 = []
+
+        def finish(g, a, b):
+            for copy in rs1[g]:
+                copy.wait_recv()
+            for h, got, q, qf, me in ((h0, r0, q0, q0f, z_me), (h1, r1, q1, q1f, y_me)):
+                for p in range(a, b):
+                    total = h[me * side + p].astype(F32)
+                    for d in range(side - 1):
+                        total = total + got[d, p].astype(F32)
+                    if p == 0:
+                        qf[...] = total
+                    else:
+                        q[p] = total.astype(BF16)
+            for p in reversed(range(max(a, 1), b)):
+                d = order[p]
+                pair = (
+                    remote(q0.at[p], t0.at[d - 1], rs2_s.at[0, d - 1], rs2_r.at[0, d - 1], at_y(along_y(d))),
+                    remote(q1.at[p], t1.at[d - 1], rs2_s.at[1, d - 1], rs2_r.at[1, d - 1], at_z(along_z(d))),
+                )
+                for copy in pair:
+                    copy.start()
+                rs2.extend(pair)
 
     with jax.named_scope("scaled"):
+        own0.wait()
+        own1.wait()
         for copy in ag2:
             copy.wait_recv()
 
         def paint(r, acc):
-            o = tab_s[base + 4, r]
             start, size = tab_s[base + 2, r] & 127, tab_s[base + 3, r]
-            first = g0[o].astype(F32).reshape(16, 128)
-            second = g1[(o & (side - 1)) * side + lax.div(o, side)].astype(F32).reshape(16, 128)
+            first = g0[tab_s[base + 4, r]].astype(F32).reshape(16, 128)
+            second = g1[tab_s[base + 6, r]].astype(F32).reshape(16, 128)
             tile = pltpu.roll(jnp.concatenate([first, second], axis=0), start, 1)
             acc = jnp.where((lane32 >= start) & (lane32 < start + size), tile, acc)
             snap[r] = acc
             return jnp.where(lane32 < start + size - 128, tile, acc)
 
-        lax.fori_loop(0, n_wide, paint, jnp.zeros((32, 128), F32), unroll=4)
+        lax.fori_loop(0, n_wide, paint, jnp.zeros((32, 128), F32), unroll=8)
+        for k in range(slots):
+            run[k, blocks] = jnp.zeros((32, 128), F32)
+
+        def link(b, _):
+            s = ens_block(b) * snap[tab_s[base + 5, b]]
+            s = halves_of([s[8 * f : 8 * f + 8] for f in range(4)]).astype(BF16).astype(F32)
+            earlier = [run[k, tab_s[slots + k, b]] for k in range(slots)]
+            for k in range(slots):
+                run[k, b] = s + earlier[k]
+            return 0
+
+        lax.fori_loop(0, blocks, link, 0, unroll=4)
+
+    with jax.named_scope("member_sum_far"):
+        for group_of in groups[2:]:
+            finish(*group_of)
+
+    with jax.named_scope("tile_product"):
         halo2 = []
         for c in range(n_groups):
 
-            def scale(i, _, c=c):
-                b = c * group + i
-                s = ens_block(b) * snap[tab_s[base + 5, b]]
-                e2[0:32, block_lanes(b)] = halves_of([s[8 * f : 8 * f + 8] for f in range(4)]).astype(BF16)
+            def pick_back(i, _, c=c):
+                j = c * group + i
+                at = pl.ds(pl.multiple_of(j * 32, 32), 32)
+                for k in range(slots):
+                    x[at, k * 128 : (k + 1) * 128] = run[k, tab_s[2 * slots + k, j]].astype(BF16)
                 return 0
 
-            lax.fori_loop(0, group, scale, 0, unroll=4)
+            lax.fori_loop(0, group, pick_back, 0, unroll=8)
+            part = lax.dot_general(
+                x[c * group * 32 : (c + 1) * group * 32, :],
+                tiles_nt[...],
+                (((1,), (1,)), ((), ())),
+                preferred_element_type=F32,
+            ).astype(BF16)
+            for i in range(group):
+                j = c * group + i
+                e2[0:32, j * 128 : (j + 1) * 128] = part[i * 32 : (i + 1) * 32]
             at = pl.ds(c * group * 128, group * 128)
             sends = [
                 remote(e2.at[0:16, at], e2.at[48:64, at], bdn_s.at[c], bdn_r.at[c], (w_me, lower)),
@@ -326,76 +410,25 @@
                 copy.start()
             halo2 += sends
 
+    with jax.named_scope("member_sum_stage_2"):
+        for group_of in reversed(groups[:2]):
+            finish(*group_of)
+
     with jax.named_scope("mix_up"):
-        for k in range(slots):
-            run[k, blocks] = jnp.zeros((32, 128), F32)
+        outs = []
+
         def up_step(i, _):
             at = pl.ds(pl.multiple_of(i * wide_mix * 128, wide_mix * 128), wide_mix * 128)
             both = jnp.dot(up, e2[:, at], preferred_element_type=F32)
-            local = (both[:32] + both[32:]).astype(BF16).astype(F32)
-            for j in range(wide_mix):
-                mixed[i * wide_mix + j] = local[:, j * 128 : (j + 1) * 128]
+            local = (both[:32] + both[32:]).astype(BF16)
+            for f in range(4):
+                grad_v[f, :, at] = local[8 * f : 8 * f + 8]
             return 0
 
         for c in range(n_groups):
             for copy in halo2[2 * c : 2 * c + 2]:
                 copy.wait_recv()
             lax.fori_loop(c * mixes, (c + 1) * mixes, up_step, 0, unroll=mixes)
-
-        def link(b, _):
-            m = mixed[b]
-            earlier = [run[k, tab_s[slots + k, b]] for k in range(slots)]
-            for k in range(slots):
-                run[k, b] = m + earlier[k]
-            return 0
-
-        lax.fori_loop(0, blocks, link, 0)
-
-    with jax.named_scope("member_sum_stage_2"):
-        for copy in rs1:
-            copy.wait_recv()
-
-        for h, got, q, qf, me in ((h0, r0, q0, q0f, z_me), (h1, r1, q1, q1f, y_me)):
-
-            def add_up(j, _, h=h, got=got, q=q, qf=qf, me=me):
-                total = h[me * side + j].astype(F32)
-                for d in range(side - 1):
-                    total = total + got[d, j].astype(F32)
-                qf[j] = total
-                q[j] = total.astype(BF16)
-                return 0
-
-            lax.fori_loop(0, side, add_up, 0, unroll=2)
-        rs2 = []
-        for d in steps:
-            z, y = along_z(d), along_y(d)
-            rs2.append(remote(q0.at[y], t0.at[d - 1], rs2_s.at[0, d - 1], rs2_r.at[0, d - 1], at_y(y)))
-            rs2.append(remote(q1.at[z], t1.at[d - 1], rs2_s.at[1, d - 1], rs2_r.at[1, d - 1], at_z(z)))
-        for copy in rs2:
-            copy.start()
-
-    with jax.named_scope("gradient"):
-        outs = []
-        for c in range(n_groups):
-
-            def pick_back(i, _, c=c):
-                j = c * group + i
-                at = pl.ds(pl.multiple_of(j * 32, 32), 32)
-                for k in range(slots):
-                    x[at, k * 128 : (k + 1) * 128] = run[k, tab_s[2 * slots + k, j]].astype(BF16)
-                return 0
-
-            lax.fori_loop(0, group, pick_back, 0, unroll=2)
-            part = lax.dot_general(
-                x[c * group * 32 : (c + 1) * group * 32, :],
-                tiles_nt[...],
-                (((1,), (1,)), ((), ())),
-                preferred_element_type=F32,
-            )
-            for i in range(group):
-                for f in range(4):
-                    j = c * group + i
-                    grad_v[f, :, j * 128 : (j + 1) * 128] = part[i * 32 + f * 8 : i * 32 + f * 8 + 8].astype(BF16)
             at = pl.ds(c * group * 128, group * 128)
             out = pltpu.make_async_copy(grad_v.at[:, :, at], grad_h.at[0, :, :, at], out_sem.at[c])
             out.start()
@@ -404,7 +437,7 @@
     with jax.named_scope("increment"):
         for copy in rs2:
             copy.wait_recv()
-        total0, total1 = q0f[y_me], q1f[z_me]
+        total0, total1 = q0f[...], q1f[...]
         for d in range(side - 1):
             total0 = total0 + t0[d].astype(F32)
             total1 = total1 + t1[d].astype(F32)
@@ -418,7 +451,8 @@
         outs.append(out)
 
     with jax.named_scope("drain"):
-        for copy in ag1 + ag2 + rs1 + rs2 + halo1 + halo2:
+        sent = [copy for pair in ag1.values() for copy in pair] + [copy for part in rs1.values() for copy in part]
+        for copy in sent + ag2 + rs2 + halo1 + halo2:
             copy.wait_send()
         for out in outs:
             out.wait()
@@ -431,6 +465,20 @@
         copy.start()
     for copy in copies:
         copy.wait()
+
+
+def hand_over(inc_h, grad_h, inc_out, grad_out, sem):
+    copies = [pltpu.make_async_copy(inc_h, inc_out, sem.at[0])]
+    copies += [pltpu.make_async_copy(grad_h.at[0, f], grad_out.at[0, f], sem.at[1 + f]) for f in range(4)]
+    for copy in copies:
+        copy.start()
+    for copy in copies:
+        copy.wait()
+
+
+def hand_over(inc_v, grad_v, inc_out, grad_out):
+    inc_out[...] = inc_v[...]
+    grad_out[...] = grad_v[...]
 
 
 def body(n_wide, n_lev, alpha, ens, htile, vloc, pattern, region_sizes, owner, cotangent):
@@ -457,15 +505,16 @@
         vmem((n_wide, 16, 128), BF16), vmem((n_wide, 16, 128), BF16),
         vmem((ring, side, 16, 128), BF16), vmem((ring, side, 16, 128), BF16),
         vmem((side, 16, 128), BF16), vmem((side, 16, 128), BF16),
-        vmem((side, 16, 128), F32), vmem((side, 16, 128), F32),
+        vmem((16, 128), F32), vmem((16, 128), F32),
         vmem((ring, 16, 128), BF16), vmem((ring, 16, 128), BF16),
         vmem((n_wide, 2, 8, 128), BF16), vmem((n_wide, 2, 8, 128), BF16),
         vmem((n_wide, 32, 128), F32),
-        vmem((blocks, 32, 128), F32),
         vmem((slots, blocks + 1, 32, 128), F32),
         vmem(alpha.shape[1:], BF16), vmem(cotangent.shape, BF16),
         dma((10,)), dma((n_groups + 1,)),
-        *[dma((2, ring))] * 8,
+        *[dma((2, ring))] * 2,
+        *[dma((2, 3, ring))] * 4,
+        *[dma((2, ring))] * 2,
         *[dma((n_groups,))] * 8,
     ]
     any_spec = pl.BlockSpec(memory_space=pl.ANY)
@@ -483,7 +532,14 @@
         alpha, ens, htile, vloc.T, pattern.T,
         region_sizes.reshape(1, n_wide), owner.reshape(1, n_wide), cotangent,
     )
-    return results
+    whole = pl.BlockSpec(memory_space=pltpu.VMEM)
+    return pl.pallas_call(
+        hand_over,
+        out_shape=shapes,
+        in_specs=[whole] * 2,
+        out_specs=(whole, whole),
+        compiler_params=pltpu.CompilerParams(vmem_limit_bytes=VMEM_LIMIT),
+    )(*results)
 
 
 def solution(mesh):

time: 44 us -> 39.8 us (0.905); the launches traced: 43.2 us -> 39.6 us
  local copies, waits for them, and re-layouts: 2.96 us -> 0 us
  Pallas kernels: 39.6 us -> 39 us
    unnamed x2 -> x0, local copies, waits for them, and re-layouts: 2.96 us -> none
    pallas_call x1, Pallas kernels: 39.6 us -> 37.3 us  [body(): pl.pallas_call(functools.partial(kernel, side, n_lev, blocks, slots, n_wi...]
    pallas_call x0 -> x1, Pallas kernels: none -> 1.69 us  [body(): pl.pallas_call(hand_over, out_shape=shapes, in_specs=[whole] * 2, out_spe...]
where the time goes in v3:
time: 39.8 us; the launch traced here: 39.6 us
  Pallas kernels  39 us (98%)
  between operations  0.64 us (2%)
    pallas_call x1, Pallas kernels, body(): pl.pallas_call(functools.partial(kernel, side, n_lev, blocks, slots, n_wi...  37.3 us
    pallas_call x1, Pallas kernels, body(): pl.pallas_call(hand_over, out_shape=shapes, in_specs=[whole] * 2, out_spe...  1.69 us

profile of v3, /device:TPU:1, one launch (start us, length us, event | category | flops | bytes accessed | tf_op | source)
XLA Modules:
  0.0 39.6 jit_solution(14009891722400737924)
XLA Ops:
  0.6 37.3 %shard_map.95 = (bf16[4,8,128]{2,1,0:T(8,128)(2,1)}, bf16[1,4,8,4096]{3,2,1,0:T(8,128)(2,1)}) custom-call(bf16[1,4,8,4096]{3,2,1,0:T(8,128)(2,1)} %alpha_h.1, bf16[1,4,8,4096]{3,2,1,0:T(8,128)(2,1)} %ens_h.1, bf16[8,128,128]{2,1,0:T(8,128)(2,1)} %htile_h.1, f32[9,64]{1,0:T(8,128)} %bitcast.4, s32[8,32]{1,0:T(8,128)} %bitcast.5, s32[1,64]{1,0:T(1,128)} %bitcast.6, ...), custom_call_target="tpu_custom_call" | custom-call | tf_op jit(solution)/shard_map/pallas_call | solution.py:522
  38.0 1.7 %shard_map.96 = (bf16[4,8,128]{2,1,0:T(8,128)(2,1)}, bf16[1,4,8,4096]{3,2,1,0:T(8,128)(2,1)}) custom-call(bf16[4,8,128]{2,1,0:T(8,128)(2,1)} %get-tuple-element.4.inc_v, bf16[1,4,8,4096]{3,2,1,0:T(8,128)(2,1)} %get-tuple-element.5.grad_v), custom_call_target="tpu_custom_call" | custom-call | tf_op jit(solution)/shard_map/pallas_call | solution.py:536

commit v4 on v3

--- a/solution.py
+++ b/solution.py
@@ -13,7 +13,7 @@
 F32 = jnp.float32
 BF16 = jnp.bfloat16
 I32 = jnp.int32
-GATHER_AFTER = 1
+GATHER_AFTER = 2
 VMEM_LIMIT = 60 * 1024 * 1024
 
 
@@ -34,8 +34,8 @@
     side, n_lev, blocks, slots, members, width,
     alpha_h, ens_h, htile_h, vloc_h, pattern_h, sizes_h, owner_h, cot_h,
     inc_h, grad_h,
-    alpha_v, ens_v, tile_v, vloc_v, pat_v, size_v, own_v, tab_v, tab_s,
-    a3, x, tiles_nt, band_v, e1, e2, p3, h0, h1, r0, r1, q0, q1, q0f, q1f, t0, t1,
+    alpha_v, ens_v, tile_v, vloc_v, pat_v, size_v, own_v, tab_v, tab_s, pat_s,
+    a3, x, tiles_t, band_v, e1, e2, p3, h0, h1, r0, r1, q0, q1, q0f, q1f, t0, t1,
     g0, g1, snap, run, grad_v, inc_v,
     local_sem, out_sem, ag1_s, ag1_r, ag2_s, ag2_r, rs1_s, rs1_r, rs2_s, rs2_r, up_s, up_r, dn_s, dn_r,
     bup_s, bup_r, bdn_s, bdn_r,
@@ -74,31 +74,34 @@
             for i, (src, dst) in enumerate(
                 (
                     (sizes_h, size_v), (owner_h, own_v), (pattern_h, pat_v),
-                    (alpha_h, alpha_v), (htile_h, tile_v), (vloc_h, vloc_v), (ens_h, ens_v),
+                    (alpha_h, alpha_v), (htile_h, tile_v), (vloc_h, vloc_v), (ens_h, ens_v), (pattern_h, pat_s),
                 )
             )
         ]
-        for load in loads:
-            load.start()
+        own0 = pltpu.make_async_copy(cot_h.at[0:2], g0.at[z_me * side], local_sem.at[8])
+        own1 = pltpu.make_async_copy(cot_h.at[2:4], g1.at[y_me * side], local_sem.at[9])
+        own0.start()
+        own1.start()
         barrier = pltpu.get_barrier_semaphore()
         friends = [at_y(along_y(d)) for d in steps] + [at_z(along_z(d)) for d in steps]
         friends += [(w_me, upper), (w_me, lower)]
         for friend in friends:
             pl.semaphore_signal(barrier, inc=1, device_id=friend, device_id_type=MESH)
+        for load in loads:
+            load.start()
 
     with jax.named_scope("cotangent_stage_1"):
-        own0 = pltpu.make_async_copy(cot_h.at[0:2], g0.at[z_me * side], local_sem.at[8])
-        own1 = pltpu.make_async_copy(cot_h.at[2:4], g1.at[y_me * side], local_sem.at[9])
-        own0.start()
-        own1.start()
+        own0.wait()
+        own1.wait()
+        mine0, mine1 = g0.at[z_me * side], g1.at[y_me * side]
         pl.semaphore_wait(barrier, len(friends))
         ag1, ag2 = {}, []
         for d in steps:
             p = place[side - d]
             to0, to1 = g0.at[z_me * side + p], g1.at[y_me * side + p]
             ag1[p] = (
-                remote(cot_h.at[0:2], to0, ag1_s.at[0, d - 1], ag1_r.at[0, d - 1], at_y(along_y(d))),
-                remote(cot_h.at[2:4], to1, ag1_s.at[1, d - 1], ag1_r.at[1, d - 1], at_z(along_z(d))),
+                remote(mine0, to0, ag1_s.at[0, d - 1], ag1_r.at[0, d - 1], at_y(along_y(d))),
+                remote(mine1, to1, ag1_s.at[1, d - 1], ag1_r.at[1, d - 1], at_z(along_z(d))),
             )
             for copy in ag1[p]:
                 copy.start()
@@ -111,12 +114,12 @@
             for d in steps:
                 pair = (
                     remote(
-                        cot_h.at[0:2] if g == 0 else g0.at[at0],
+                        mine0 if g == 0 else g0.at[at0],
                         g0.at[z_me * side] if g == 0 else g0.at[at0],
                         ag2_s.at[0, g, d - 1], ag2_r.at[0, g, d - 1], at_z(along_z(d)),
                     ),
                     remote(
-                        cot_h.at[2:4] if g == 0 else g1.at[at1],
+                        mine1 if g == 0 else g1.at[at1],
                         g1.at[y_me * side] if g == 0 else g1.at[at1],
                         ag2_s.at[1, g, d - 1], ag2_r.at[1, g, d - 1], at_y(along_y(d)),
                     ),
@@ -127,49 +130,6 @@
 
         forward(*groups[0])
 
-    with jax.named_scope("tables"):
-        for load in loads[:3]:
-            load.wait()
-        square = (n_wide, n_wide)
-        rows, cols = iota(square, 0), iota(square, 1)
-        size_b = jnp.broadcast_to(size_v[...], square)
-        own_b = jnp.broadcast_to(own_v[...], square)
-        start_c = jnp.sum(jnp.where(cols < rows, size_b, 0), axis=1, keepdims=True)
-        size_c = jnp.sum(jnp.where(cols == rows, size_b, 0), axis=1, keepdims=True)
-        own_c = jnp.sum(jnp.where(cols == rows, own_b, 0), axis=1, keepdims=True)
-        held = own_c == cols
-        base = 3 * slots
-        tab_v[base : base + 1, 0:n_wide] = jnp.sum(jnp.where(held, start_c, 0), axis=0, keepdims=True)
-        tab_v[base + 1 : base + 2, 0:n_wide] = jnp.sum(jnp.where(held, size_c, 0), axis=0, keepdims=True)
-        tab_v[base + 2 : base + 3, 0:n_wide] = jnp.sum(jnp.where(cols == rows, start_c, 0), axis=0, keepdims=True)
-        tab_v[base + 3 : base + 4, 0:n_wide] = size_v[...]
-
-
-        def near(d):
-            return jnp.where(2 * d <= side, jnp.maximum(2 * d - 1, 0), 2 * (side - d))
-
-        z_own, y_own = lax.shift_right_logical(own_v[...], bits), own_v[...] & (side - 1)
-        tab_v[base + 4 : base + 5, 0:n_wide] = z_own * side + near((y_own - y_me) & (side - 1))
-        tab_v[base + 6 : base + 7, 0:n_wide] = y_own * side + near((z_own - z_me) & (side - 1))
-        ends = iota((n_wide, blocks), 1) * 128 + 127
-        covered = jnp.sum(jnp.where(start_c + size_c <= ends, 1, 0), axis=0, keepdims=True)
-        tab_v[base + 5 : base + 6, 0:blocks] = jnp.minimum(covered, n_wide - 1)
-        here, there = iota((blocks, blocks), 0), iota((blocks, blocks), 1)
-        for k in range(slots):
-            row = pat_v[k : k + 1, :]
-            col = jnp.sum(jnp.where(here == there, row, 0), axis=1, keepdims=True)
-            tab_v[k : k + 1, 0:blocks] = row
-            before = jnp.max(jnp.where((col == row) & (here < there), here, -1), axis=0, keepdims=True)
-            tab_v[slots + k : slots + k + 1, 0:blocks] = jnp.where(before < 0, blocks, before)
-            last = jnp.max(jnp.where(col == there, here, -1), axis=0, keepdims=True)
-            tab_v[2 * slots + k : 2 * slots + k + 1, 0:blocks] = jnp.where(last < 0, blocks, last)
-        to_s = pltpu.make_async_copy(tab_v, tab_s, local_sem.at[7])
-        to_s.start()
-        to_s.wait()
-        my_start = tab_s[base, w_me]
-        my_size = tab_s[base + 1, w_me]
-        my_off = my_start & 127
-
     lane16, lane32 = iota((16, 128), 1), iota((32, 128), 1)
 
     def block_lanes(b):
@@ -177,6 +137,7 @@
 
     with jax.named_scope("spread"):
         loads[3].wait()
+        loads[7].wait()
 
         def split_alpha(b, _):
             a = alpha_v[0, :, :, block_lanes(b)].astype(F32)
@@ -195,7 +156,7 @@
                 b = c * group + i
                 at = pl.ds(pl.multiple_of(b * 32, 32), 32)
                 for k in range(slots):
-                    x[at, k * 128 : (k + 1) * 128] = a3[tab_s[k, b]]
+                    x[at, k * 128 : (k + 1) * 128] = a3[pat_s[k, b]]
                 return 0
 
             lax.fori_loop(0, group, pick, 0, unroll=8)
@@ -217,6 +178,49 @@
                 for group_of in groups[1:2]:
                     forward(*group_of)
 
+    with jax.named_scope("cotangent_stage_2"):
+        for group_of in groups[2:]:
+            forward(*group_of)
+
+    with jax.named_scope("tables"):
+        for load in loads[:3]:
+            load.wait()
+        square = (n_wide, n_wide)
+        rows, cols = iota(square, 0), iota(square, 1)
+        size_b = jnp.broadcast_to(size_v[...], square)
+        own_b = jnp.broadcast_to(own_v[...], square)
+        start_c = jnp.sum(jnp.where(cols < rows, size_b, 0), axis=1, keepdims=True)
+        size_c = jnp.sum(jnp.where(cols == rows, size_b, 0), axis=1, keepdims=True)
+        own_c = jnp.sum(jnp.where(cols == rows, own_b, 0), axis=1, keepdims=True)
+        held = own_c == cols
+        base = 3 * slots
+        tab_v[base : base + 1, 0:n_wide] = jnp.sum(jnp.where(held, start_c, 0), axis=0, keepdims=True)
+        tab_v[base + 1 : base + 2, 0:n_wide] = jnp.sum(jnp.where(held, size_c, 0), axis=0, keepdims=True)
+        tab_v[base + 2 : base + 3, 0:n_wide] = jnp.sum(jnp.where(cols == rows, start_c, 0), axis=0, keepdims=True)
+        tab_v[base + 3 : base + 4, 0:n_wide] = size_v[...]
+
+
+        def near(d):
+            return jnp.where(2 * d <= side, jnp.maximum(2 * d - 1, 0), 2 * (side - d))
+
+        z_own, y_own = lax.shift_right_logical(own_v[...], bits), own_v[...] & (side - 1)
+        tab_v[base + 4 : base + 5, 0:n_wide] = z_own * side + near((y_own - y_me) & (side - 1))
+        tab_v[base + 6 : base + 7, 0:n_wide] = y_own * side + near((z_own - z_me) & (side - 1))
+        ends = iota((n_wide, blocks), 1) * 128 + 127
+        covered = jnp.sum(jnp.where(start_c + size_c <= ends, 1, 0), axis=0, keepdims=True)
+        tab_v[base + 5 : base + 6, 0:blocks] = jnp.minimum(covered, n_wide - 1)
+        here, there = iota((blocks, blocks), 0), iota((blocks, blocks), 1)
+        for k in range(slots):
+            row = pat_v[k : k + 1, :]
+            col = jnp.sum(jnp.where(here == there, row, 0), axis=1, keepdims=True)
+            tab_v[k : k + 1, 0:blocks] = row
+            before = jnp.max(jnp.where((col == row) & (here < there), here, -1), axis=0, keepdims=True)
+            tab_v[slots + k : slots + k + 1, 0:blocks] = jnp.where(before < 0, blocks, before)
+            last = jnp.max(jnp.where(col == there, here, -1), axis=0, keepdims=True)
+            tab_v[2 * slots + k : 2 * slots + k + 1, 0:blocks] = jnp.where(last < 0, blocks, last)
+        to_s = pltpu.make_async_copy(tab_v, tab_s, local_sem.at[10])
+        to_s.start()
+
     with jax.named_scope("bands"):
         loads[5].wait()
         first_level = l_me * 8
@@ -262,8 +266,10 @@
         rows_in = [lows, lows, highs, highs, before, before, after, after] + [jnp.zeros((8, width), F32)] * 8
         up = banded(jnp.concatenate(rows_in, axis=0), inside, level_out - level_in + REACH)
         up = in_two(jnp.transpose(up)[0:32, 0:64])
-        for group_of in groups[2:]:
-            forward(*group_of)
+        to_s.wait()
+        my_start = tab_s[base, w_me]
+        my_size = tab_s[base + 1, w_me]
+        my_off = my_start & 127
 
     with jax.named_scope("ensemble"):
         loads[6].wait()
@@ -272,7 +278,7 @@
             return ens_v[0, :, :, block_lanes(b)].astype(F32).reshape(32, 128)
 
         for k in range(slots):
-            tiles_nt[:, k * 128 : (k + 1) * 128] = tile_v[k]
+            tiles_t[k * 128 : (k + 1) * 128, :] = jnp.transpose(tile_v[k].astype(F32)).astype(BF16)
 
     with jax.named_scope("mix_down"):
         wide_mix = min(4, blocks)
@@ -348,8 +354,6 @@
                 rs2.extend(pair)
 
     with jax.named_scope("scaled"):
-        own0.wait()
-        own1.wait()
         for copy in ag2:
             copy.wait_recv()
 
@@ -392,11 +396,8 @@
                 return 0
 
             lax.fori_loop(0, group, pick_back, 0, unroll=8)
-            part = lax.dot_general(
-                x[c * group * 32 : (c + 1) * group * 32, :],
-                tiles_nt[...],
-                (((1,), (1,)), ((), ())),
-                preferred_element_type=F32,
+            part = jnp.dot(
+                x[c * group * 32 : (c + 1) * group * 32, :], tiles_t[...], preferred_element_type=F32
             ).astype(BF16)
             for i in range(group):
                 j = c * group + i
@@ -409,10 +410,11 @@
             for copy in sends:
                 copy.start()
             halo2 += sends
+            if c == max(n_groups - 2, 0):
+                finish(*groups[1])
 
     with jax.named_scope("member_sum_stage_2"):
-        for group_of in reversed(groups[:2]):
-            finish(*group_of)
+        finish(*groups[0])
 
     with jax.named_scope("mix_up"):
         outs = []
@@ -458,27 +460,17 @@
             out.wait()
 
 
-def hand_over(inc_h, grad_h, inc_out, grad_out, sem):
-    copies = [pltpu.make_async_copy(inc_h, inc_out, sem.at[0])]
-    copies += [pltpu.make_async_copy(grad_h.at[0, f], grad_out.at[0, f], sem.at[1 + f]) for f in range(4)]
-    for copy in copies:
-        copy.start()
-    for copy in copies:
-        copy.wait()
-
-
-def hand_over(inc_h, grad_h, inc_out, grad_out, sem):
-    copies = [pltpu.make_async_copy(inc_h, inc_out, sem.at[0])]
-    copies += [pltpu.make_async_copy(grad_h.at[0, f], grad_out.at[0, f], sem.at[1 + f]) for f in range(4)]
-    for copy in copies:
-        copy.start()
-    for copy in copies:
-        copy.wait()
-
-
-def hand_over(inc_v, grad_v, inc_out, grad_out):
-    inc_out[...] = inc_v[...]
-    grad_out[...] = grad_v[...]
+def hand_over(inc_h, grad_h, inc_out, grad_out, inc_v, grad_v, sem_in, sem_out):
+    parts = [(grad_h.at[0, f], grad_v.at[f], grad_out.at[0, f]) for f in range(4)] + [(inc_h, inc_v, inc_out)]
+    reads = [pltpu.make_async_copy(src, mid, sem_in.at[i]) for i, (src, mid, _) in enumerate(parts)]
+    writes = [pltpu.make_async_copy(mid, dst, sem_out.at[i]) for i, (_, mid, dst) in enumerate(parts)]
+    for read in reads:
+        read.start()
+    for read, write in zip(reads, writes):
+        read.wait()
+        write.start()
+    for write in writes:
+        write.wait()
 
 
 def body(n_wide, n_lev, alpha, ens, htile, vloc, pattern, region_sizes, owner, cotangent):
@@ -496,9 +488,10 @@
         vmem(alpha.shape, BF16), vmem(ens.shape, BF16), vmem(htile.shape, BF16), vmem(vloc.shape[::-1], F32),
         vmem(pattern.shape[::-1], I32), vmem((1, n_wide), I32), vmem((1, n_wide), I32),
         vmem((32, 128), I32), pltpu.SMEM((32, 128), I32),
+        pltpu.SMEM(pattern.shape[::-1], I32),
         vmem((blocks, 32, 128), BF16),
         vmem((blocks * 32, slots * 128), BF16),
-        vmem((128, slots * 128), BF16),
+        vmem((slots * 128, 128), BF16),
         vmem(vloc.shape, F32),
         vmem((64, columns), BF16), vmem((64, columns), BF16),
         vmem((blocks, 32, 128), F32),
@@ -511,7 +504,7 @@
         vmem((n_wide, 32, 128), F32),
         vmem((slots, blocks + 1, 32, 128), F32),
         vmem(alpha.shape[1:], BF16), vmem(cotangent.shape, BF16),
-        dma((10,)), dma((n_groups + 1,)),
+        dma((11,)), dma((n_groups + 1,)),
         *[dma((2, ring))] * 2,
         *[dma((2, 3, ring))] * 4,
         *[dma((2, ring))] * 2,
@@ -532,12 +525,12 @@
         alpha, ens, htile, vloc.T, pattern.T,
         region_sizes.reshape(1, n_wide), owner.reshape(1, n_wide), cotangent,
     )
-    whole = pl.BlockSpec(memory_space=pltpu.VMEM)
     return pl.pallas_call(
         hand_over,
         out_shape=shapes,
-        in_specs=[whole] * 2,
-        out_specs=(whole, whole),
+        in_specs=[any_spec] * 2,
+        out_specs=(any_spec, any_spec),
+        scratch_shapes=[vmem(cotangent.shape, BF16), vmem(alpha.shape[1:], BF16), dma((5,)), dma((5,))],
         compiler_params=pltpu.CompilerParams(vmem_limit_bytes=VMEM_LIMIT),
     )(*results)
 

time: 39.8 us -> 38.9 us (0.977)
  Pallas kernels: 39 us -> 38.1 us
    pallas_call x1, Pallas kernels: 37.3 us -> 36.4 us  [body(): pl.pallas_call(functools.partial(kernel, side, n_lev, blocks, slots, n_wi...]
where the time goes in v4:
time: 38.9 us; the launch traced here: 38.7 us
  Pallas kernels  38.1 us (98%)
  between operations  0.64 us (2%)
    pallas_call x1, Pallas kernels, body(): pl.pallas_call(functools.partial(kernel, side, n_lev, blocks, slots, n_wi...  36.4 us
    pallas_call x1, Pallas kernels, body(): pl.pallas_call(hand_over, out_shape=shapes, in_specs=[any_spec] * 2, out_...  1.65 us

profile of v4, /device:TPU:1, one launch (start us, length us, event | category | flops | bytes accessed | tf_op | source)
XLA Modules:
  0.0 38.7 jit_solution(5127192264083013858)
XLA Ops:
  0.6 36.4 %shard_map.95 = (bf16[4,8,128]{2,1,0:T(8,128)(2,1)}, bf16[1,4,8,4096]{3,2,1,0:T(8,128)(2,1)}) custom-call(bf16[1,4,8,4096]{3,2,1,0:T(8,128)(2,1)} %alpha_h.1, bf16[1,4,8,4096]{3,2,1,0:T(8,128)(2,1)} %ens_h.1, bf16[8,128,128]{2,1,0:T(8,128)(2,1)} %htile_h.1, f32[9,64]{1,0:T(8,128)} %bitcast.4, s32[8,32]{1,0:T(8,128)} %bitcast.5, s32[1,64]{1,0:T(1,128)} %bitcast.6, ...), custom_call_target="tpu_custom_call" | custom-call | tf_op jit(solution)/shard_map/pallas_call | solution.py:515
  37.1 1.7 %shard_map.96 = (bf16[4,8,128]{2,1,0:T(8,128)(2,1)}, bf16[1,4,8,4096]{3,2,1,0:T(8,128)(2,1)}) custom-call(bf16[4,8,128]{2,1,0:T(8,128)(2,1)} %get-tuple-element.4.inc_h, bf16[1,4,8,4096]{3,2,1,0:T(8,128)(2,1)} %get-tuple-element.5.grad_h), custom_call_target="tpu_custom_call" | custom-call | tf_op jit(solution)/shard_map/pallas_call | solution.py:528

commit v5 on v4

--- a/solution.py
+++ b/solution.py
@@ -128,7 +128,6 @@
                     copy.start()
                 ag2.extend(pair)
 
-        forward(*groups[0])
 
     lane16, lane32 = iota((16, 128), 1), iota((32, 128), 1)
 
@@ -174,6 +173,8 @@
             for copy in sends:
                 copy.start()
             halo1 += sends
+            if c == 0:
+                forward(*groups[0])
             if c == min(GATHER_AFTER, n_groups - 1):
                 for group_of in groups[1:2]:
                     forward(*group_of)
@@ -380,10 +381,6 @@
 
         lax.fori_loop(0, blocks, link, 0, unroll=4)
 
-    with jax.named_scope("member_sum_far"):
-        for group_of in groups[2:]:
-            finish(*group_of)
-
     with jax.named_scope("tile_product"):
         halo2 = []
         for c in range(n_groups):
@@ -410,7 +407,10 @@
             for copy in sends:
                 copy.start()
             halo2 += sends
-            if c == max(n_groups - 2, 0):
+            if c == 0:
+                for group_of in groups[2:]:
+                    finish(*group_of)
+            if c == n_groups - 1:
                 finish(*groups[1])
 
     with jax.named_scope("member_sum_stage_2"):

time: 38.9 us -> 39 us (level)
  no operation moved by 1% of the time
where the time goes in v5:
time: 39 us; the launch traced here: 38.8 us
  Pallas kernels  38.1 us (98%)
  between operations  0.64 us (2%)
    pallas_call x1, Pallas kernels, body(): pl.pallas_call(functools.partial(kernel, side, n_lev, blocks, slots, n_wi...  36.5 us
    pallas_call x1, Pallas kernels, body(): pl.pallas_call(hand_over, out_shape=shapes, in_specs=[any_spec] * 2, out_...  1.65 us

profile of v5, /device:TPU:1, one launch (start us, length us, event | category | flops | bytes accessed | tf_op | source)
XLA Modules:
  0.0 38.8 jit_solution(13805979002027099087)
XLA Ops:
  0.6 36.5 %shard_map.95 = (bf16[4,8,128]{2,1,0:T(8,128)(2,1)}, bf16[1,4,8,4096]{3,2,1,0:T(8,128)(2,1)}) custom-call(bf16[1,4,8,4096]{3,2,1,0:T(8,128)(2,1)} %alpha_h.1, bf16[1,4,8,4096]{3,2,1,0:T(8,128)(2,1)} %ens_h.1, bf16[8,128,128]{2,1,0:T(8,128)(2,1)} %htile_h.1, f32[9,64]{1,0:T(8,128)} %bitcast.4, s32[8,32]{1,0:T(8,128)} %bitcast.5, s32[1,64]{1,0:T(1,128)} %bitcast.6, ...), custom_call_target="tpu_custom_call" | custom-call | tf_op jit(solution)/shard_map/pallas_call | solution.py:515
  37.1 1.7 %shard_map.96 = (bf16[4,8,128]{2,1,0:T(8,128)(2,1)}, bf16[1,4,8,4096]{3,2,1,0:T(8,128)(2,1)}) custom-call(bf16[4,8,128]{2,1,0:T(8,128)(2,1)} %get-tuple-element.4.inc_h, bf16[1,4,8,4096]{3,2,1,0:T(8,128)(2,1)} %get-tuple-element.5.grad_h), custom_call_target="tpu_custom_call" | custom-call | tf_op jit(solution)/shard_map/pallas_call | solution.py:528

commit v6 on v4

--- a/solution.py
+++ b/solution.py
@@ -128,7 +128,6 @@
                     copy.start()
                 ag2.extend(pair)
 
-        forward(*groups[0])
 
     lane16, lane32 = iota((16, 128), 1), iota((32, 128), 1)
 
@@ -174,6 +173,8 @@
             for copy in sends:
                 copy.start()
             halo1 += sends
+            if c == 0:
+                forward(*groups[0])
             if c == min(GATHER_AFTER, n_groups - 1):
                 for group_of in groups[1:2]:
                     forward(*group_of)

time: 38.9 us -> 39 us (level)
  no operation moved by 1% of the time
where the time goes in v6:
time: 39 us; the launch traced here: 38.8 us
  Pallas kernels  38.1 us (98%)
  between operations  0.64 us (2%)
    pallas_call x1, Pallas kernels, body(): pl.pallas_call(functools.partial(kernel, side, n_lev, blocks, slots, n_wi...  36.5 us
    pallas_call x1, Pallas kernels, body(): pl.pallas_call(hand_over, out_shape=shapes, in_specs=[any_spec] * 2, out_...  1.65 us

profile of v6, /device:TPU:1, one launch (start us, length us, event | category | flops | bytes accessed | tf_op | source)
XLA Modules:
  0.0 38.8 jit_solution(521854072776170838)
XLA Ops:
  0.6 36.5 %shard_map.95 = (bf16[4,8,128]{2,1,0:T(8,128)(2,1)}, bf16[1,4,8,4096]{3,2,1,0:T(8,128)(2,1)}) custom-call(bf16[1,4,8,4096]{3,2,1,0:T(8,128)(2,1)} %alpha_h.1, bf16[1,4,8,4096]{3,2,1,0:T(8,128)(2,1)} %ens_h.1, bf16[8,128,128]{2,1,0:T(8,128)(2,1)} %htile_h.1, f32[9,64]{1,0:T(8,128)} %bitcast.4, s32[8,32]{1,0:T(8,128)} %bitcast.5, s32[1,64]{1,0:T(1,128)} %bitcast.6, ...), custom_call_target="tpu_custom_call" | custom-call | tf_op jit(solution)/shard_map/pallas_call | solution.py:516
  37.1 1.7 %shard_map.96 = (bf16[4,8,128]{2,1,0:T(8,128)(2,1)}, bf16[1,4,8,4096]{3,2,1,0:T(8,128)(2,1)}) custom-call(bf16[4,8,128]{2,1,0:T(8,128)(2,1)} %get-tuple-element.4.inc_h, bf16[1,4,8,4096]{3,2,1,0:T(8,128)(2,1)} %get-tuple-element.5.grad_h), custom_call_target="tpu_custom_call" | custom-call | tf_op jit(solution)/shard_map/pallas_call | solution.py:529
